TPU v7x, 256 devices: a whole 4x4x8 slice. The times are simulated.
256 devices in a mesh: chan: 16 (over y_lo, z), seg: 16 (over y_hi, x, core).
Axes of the slice: x: 4, y: 4 (y_hi: 2, y_lo: 2; y = y_hi * 2 + y_lo), z: 8, core: 2. Of those that a mesh axis runs over, the one named last changes fastest.
Arguments:
- traces: bfloat16 [2048, 32768], P('chan', 'seg'), may hold values from -36 to 36
- pair_bins: int32 [2, 2048, 128], P(None, 'chan'), may hold values from 0 to 255
Outputs:
- correlograms: float32 [65, 256], P(None, 'chan')
All inputs are finite; a program needn't handle non-finite values.
Results may differ from a plain program's by a relative error of at most 0.0029.
Values may be sent and summed in bfloat16 or wider, within the bound.
No kernel may reach another device: no remote copies, remote signals or barrier semaphores. Data moves between devices by JAX's collectives and lax.ppermute only.
A program may use at most 64 MiB of HBM per device.

v0:
```python
import math

import jax
import jax.numpy as jnp
from jax import lax
from jax.sharding import PartitionSpec as P

MAX_LAG = 32
NB = 256
ROUNDS = 2


EPSILON = 1e-06
LAG_GROUP = 13


def from_behind(block, axis, distance):
    devices = range(lax.axis_size(axis))
    route = [((i - distance) % len(devices), i) for i in devices]
    return lax.ppermute(block, axis, route)


def round_stack(own_block, own_scale, partner, partner_scale, round_bins, time_scale):
    channels, seg_length = own_block.shape
    lag_count = 2 * MAX_LAG + 1
    padded = jnp.pad(partner, ((0, 0), (MAX_LAG, MAX_LAG)))

    def lag_block(carry, group_index):
        window = lax.dynamic_slice_in_dim(
            padded, group_index * LAG_GROUP, seg_length + LAG_GROUP - 1, 1
        )
        pieces = []
        for offset in range(LAG_GROUP):
            shifted = window[:, offset : offset + seg_length]
            pieces.append(
                lax.dot_general(
                    own_block, shifted, (((1,), (1,)), ((), ())), preferred_element_type=jnp.float32
                )
            )
        return (carry, jnp.stack(pieces, 0))

    _, grouped = lax.scan(lag_block, 0, jnp.arange(lag_count // LAG_GROUP, dtype=jnp.int32))
    raw_sums = grouped.reshape(lag_count, channels, channels)
    zscore = raw_sums * own_scale[None, :, None] * partner_scale[None, None, :] * time_scale
    flat_scores = zscore.astype(jnp.bfloat16).reshape(lag_count, channels * channels)
    row_block = min(16, channels)
    width = row_block * channels
    bin_ids = jnp.arange(NB, dtype=jnp.int32)
    flat_bins = round_bins.reshape(channels * channels)

    def bin_step(running, block_index):
        score_piece = lax.dynamic_slice_in_dim(flat_scores, block_index * width, width, 1)
        bin_piece = lax.dynamic_slice_in_dim(flat_bins, block_index * width, width, 0)
        onehot = (bin_piece[:, None] == bin_ids[None, :]).astype(jnp.bfloat16)
        return (running + jnp.dot(score_piece, onehot, preferred_element_type=jnp.float32), None)

    running = jnp.zeros((lag_count, NB), jnp.float32)
    running, _ = lax.scan(bin_step, running, jnp.arange(channels // row_block, dtype=jnp.int32))
    return running


def squares(block):
    return jnp.sum(jnp.square(block.astype(jnp.float32)), axis=1)


def local(traces, pair_bins):
    channels, seg_length = traces.shape
    chan_count = lax.axis_size("chan")
    seg_count = lax.axis_size("seg")
    total_time = seg_length * seg_count
    time_scale = 1.0 / math.sqrt(total_time)
    half_loop = chan_count // 2
    far_block = from_behind(traces, "chan", -half_loop)
    near_block = from_behind(traces, "chan", 1 - half_loop)
    stacked = jnp.stack([squares(traces), squares(far_block), squares(near_block)], 0)
    energies = lax.psum(stacked, "seg")
    scales = lax.rsqrt(energies / total_time + EPSILON)
    partial_value = round_stack(traces, scales[0], far_block, scales[1], pair_bins[0], time_scale)
    partial_value = partial_value + round_stack(
        traces, scales[0], near_block, scales[2], pair_bins[1], time_scale
    )
    summed = lax.psum(partial_value, "seg")
    owned = lax.psum_scatter(summed, "chan", scatter_dimension=1, tiled=True)
    pair_total = ROUNDS * chan_count * channels * channels // NB
    return owned * (1.0 / math.sqrt(pair_total))


def solution(mesh):
    in_specs = (P("chan", "seg"), P(None, "chan", None))
    out_specs = P(None, "chan")
    return jax.shard_map(local, mesh=mesh, in_specs=in_specs, out_specs=out_specs, check_vma=False)
```

profile of v0, /device:TPU:1, one launch (start us, length us, event | category | flops | bytes accessed | tf_op | source)
XLA Modules:
  0.0 343.4 jit_solution(4014678541879753089)
XLA Ops:
  6.5 2.1 collective-permute-start
  8.7 1.5 collective-permute-start.1
  10.2 1.3 multiply_reduce_fusion.2
  11.5 0.9 slice_bitcast_fusion
  12.3 7.0 %collective-permute-done = bf16[128,2048]{1,0:T(8,128)(2,1)S(1)} collective-permute-done((bf16[128,2048]{1,0:T(8,128)(2,1)}, bf16[128,2048]{1,0:T(8,128)(2,1)S(1)}, u32[]{:S(2)}, u32[]{:S(2)}) %collective-permute-start) | collective-permute-done | bytes 524320 | tf_op jit(solution)/shard_map/ppermute | solution.py:20
  19.5 6.3 %collective-permute-done.1 = bf16[128,2048]{1,0:T(8,128)(2,1)S(1)} collective-permute-done((bf16[128,2048]{1,0:T(8,128)(2,1)}, bf16[128,2048]{1,0:T(8,128)(2,1)S(1)}, u32[]{:S(2)}, u32[]{:S(2)}) %collective-permute-start.1) | collective-permute-done | bytes 524320 | tf_op jit(solution)/shard_map/ppermute | solution.py:20
  26.0 34.1 %psum.14 = f32[3,128]{1,0:T(4,128)S(1)} all-reduce(f32[3,128]{1,0:T(4,128)S(1)} %pad_maximum_fusion), channel_id=1, replica_groups=mesh['chan'=16,'seg'=16] {'seg'}, use_global_device_ids=true, to_apply=%region_5.6 | all-reduce | flops 384 | bytes 3072 | tf_op jit(solution)/shard_map/psum | solution.py:76
  60.4 2.5 broadcast.29.clone2.1
  62.9 38.1 %while.42 = (s32[]{:T(128)}, f32[5,13,128,128]{3,2,1,0:T(8,128)}, s32[5]{0:T(128)S(1)}, bf16[128,2112]{1,0:T(8,128)(2,1)S(1)}, bf16[128,2048]{1,0:T(8,128)(2,1)S...) while((s32[]{:T(128)}, f32[5,13,128,128]{3,2,1,0:T(8,128)}, ...), condition=%wide.region_1.0_spmd, body=%wide.region_0.0_spmd.sunk | while | flops 872415232 | bytes 17892284 | solution.py:42
  62.9 0.6 dynamic_slice.50
  69.5 1.0 constant_dynamic-update-slice_fusion.4
  70.5 0.6 dynamic_slice.50
  77.1 1.0 constant_dynamic-update-slice_fusion.4
  78.1 0.6 dynamic_slice.50
  84.8 1.0 constant_dynamic-update-slice_fusion.4
  85.7 0.6 dynamic_slice.50
  92.4 1.0 constant_dynamic-update-slice_fusion.4
  93.3 0.6 dynamic_slice.50
  100.0 1.0 constant_dynamic-update-slice_fusion.4
  101.0 2.9 pad.12
  103.9 4.8 %copy.22 = f32[9,8,128,128]{3,1,2,0:T(8,128)} copy(f32[9,8,128,128]{3,2,1,0:T(8,128)S(1)} %bitcast.340) | data formatting | bytes 9437184
  109.0 2.6 broadcast.29.clone2
  111.5 37.8 %while.43 = (s32[]{:T(128)}, f32[5,13,128,128]{3,2,1,0:T(8,128)}, s32[5]{0:T(128)S(1)}, bf16[128,2112]{1,0:T(8,128)(2,1)S(1)}, bf16[128,2048]{1,0:T(8,128)(2,1)S...) while((s32[]{:T(128)}, f32[5,13,128,128]{3,2,1,0:T(8,128)}, ...), condition=%wide.region_9.10_spmd, body=%wide.region_8.9_spmd.sunk | while | flops 872415232 | bytes 17892284 | solution.py:42
  111.5 0.6 dynamic_slice.51
  118.1 1.0 constant_dynamic-update-slice_fusion.5
  119.1 0.6 dynamic_slice.51
  125.7 1.0 constant_dynamic-update-slice_fusion.5
  133.2 1.0 constant_dynamic-update-slice_fusion.5
  140.8 1.0 constant_dynamic-update-slice_fusion.5
  148.3 1.0 constant_dynamic-update-slice_fusion.5
  149.4 3.1 pad.13
  152.5 2.7 copy.23
  155.3 2.6 multiply_convert_fusion
  158.0 23.3 %while.45 = (s32[]{:T(128)}, f32[65,256]{1,0:T(8,128)S(1)}, s32[8]{0:T(128)S(1)}, bf16[65,16384]{1,0:T(8,128)(2,1)}, s32[16384]{0:T(1024)S(1)}, /*index=5*/s32[]{:T(128)}, s32[1]{0:T(128)}, s32[]{:T(128)}, s32[]{:T(128)}) while((s32[]{:T(128)}, f32[65,256]{1,0:T(8,128)S(1)}, s32[8]{0:T(128)S(1)}, bf16[65,16384]{1,0:T(8,128)(2,1)}, ...), condition=%wide.region_11.12_spmd.clone, body=%wide.region_10.11_spmd.clone.sunk | while | flops 68715016 | bytes 452777 | solution.py:58
  158.0 0.6 dynamic_slice.56
  159.3 1.5 fusion.281
  160.9 0.7 dynamic_slice.56
  162.2 1.5 fusion.281
  163.8 0.7 dynamic_slice.56
  165.2 1.5 fusion.281
  166.7 0.7 dynamic_slice.56
  168.1 1.5 fusion.281
  169.6 0.7 dynamic_slice.56
  171.0 1.5 fusion.281
  172.6 0.7 dynamic_slice.56
  173.9 1.5 fusion.281
  175.5 0.7 dynamic_slice.56
  176.8 1.5 fusion.281
  178.4 0.7 dynamic_slice.56
  179.8 1.5 fusion.281
  181.3 15.2 %while.44 = (s32[]{:T(128)}, f32[65,256]{1,0:T(8,128)S(1)}, s32[8]{0:T(128)S(1)}, bf16[65,16384]{1,0:T(8,128)(2,1)S(1)}, s32[16384]{0:T(1024)S(1)}, /*index=5*/s32[]{:T(128)}, s32[1]{0:T(128)}, s32[]{:T(128)}, s32[]{:T(128)}) while((s32[]{:T(128)}, f32[65,256]{1,0:T(8,128)S(1)}, s32[8]{0:T(128)S(1)}, ...), condition=%wide.region_7.8_spmd.clone, body=%wide.region_6.7_spmd.clone.sunk | while | flops 68715016 | bytes 459945 | solution.py:58
  181.3 0.7 dynamic_slice.53
  183.2 0.7 dynamic_slice.53
  185.1 0.7 dynamic_slice.53
  187.1 0.7 dynamic_slice.53
  189.0 0.7 dynamic_slice.53
  190.9 0.7 dynamic_slice.53
  192.8 0.7 dynamic_slice.53
  194.7 0.7 dynamic_slice.53
  196.6 0.8 copy.13
  197.4 66.0 %reduce-scatter.4.cloned.1.call-done = f32[16,65]{1,0:T(8,128)} async-done(((f32[256,65]{1,0:T(8,128)}), f32[16,65]{1,0:T(8,128)}) %reduce-scatter.4.cloned.1.call-update) | async-done | bytes 4176
  263.4 0.8 copy.14
  264.2 71.7 %psum.16 = f32[65,16]{1,0:T(8,128)S(1)} all-reduce(f32[65,16]{1,0:T(8,128)S(1)} %copy.14), channel_id=1, replica_groups=mesh['chan'=16,'seg'=16] {'seg'}, use_global_device_ids=true, to_apply=%region_12.13 | all-reduce | flops 1040 | bytes 8320 | tf_op jit(solution)/shard_map/psum | solution.py:82
  335.9 0.7 copy.12
  (197 shorter events, 60.4 us)
Async XLA Ops:
  6.5 56.4 %copy-start = (bf16[128,2048]{1,0:T(8,128)(2,1)S(1)}, bf16[128,2048]{1,0:T(8,128)(2,1)}, u32[]{:S(2)}) copy-start(bf16[128,2048]{1,0:T(8,128)(2,1)} %param.10) | copy-start | bytes 1572868
  6.5 256.8 %reduce-scatter.4.cloned.1.call-start = ((), (), s32[]{:S(2)}) async-start(), calls=%async_computation.1 | async-start | bytes 139264
  6.5 12.8 %collective-permute-start = (bf16[128,2048]{1,0:T(8,128)(2,1)}, bf16[128,2048]{1,0:T(8,128)(2,1)S(1)}, u32[]{:S(2)}, u32[]{:S(2)}) collective-permute-start(bf16[128,2048]{1,0:T(8,128)(2,1)} %param.10), channel_id=1, source_target_pairs={{128,0},{144,16},{160,32},{176,48},{192,64},{208,80},{224,96},{240... | collective-permute-start | bytes 1572872 | tf_op jit(solution)/shard_map/ppermute | solution.py:20
  8.7 17.1 %collective-permute-start.1 = (bf16[128,2048]{1,0:T(8,128)(2,1)}, bf16[128,2048]{1,0:T(8,128)(2,1)S(1)}, u32[]{:S(2)}, u32[]{:S(2)}) collective-permute-start(bf16[128,2048]{1,0:T(8,128)(2,1)} %param.10), channel_id=1, source_target_pairs={{112,0},{128,16},{144,32},{160,48},{176,64},{192,80},{208,96},{224... | collective-permute-start | bytes 1572872 | tf_op jit(solution)/shard_map/ppermute | solution.py:20
  149.4 5.9 %slice-start = ((s8[4718592]{0:T(1024)(128)(4,1)}), s8[4194304]{0:T(1024)(128)(4,1)S(1)}, s32[]{:S(2)}) async-start(s8[4718592]{0:T(1024)(128)(4,1)} %bitcast.335), calls=%async_computation.2 | async-start | bytes 8388608
  152.5 2.8 slice-start.1
  155.3 2.7 copy-start.2
  158.0 23.4 %copy-start.1 = (f32[65,256]{1,0:T(8,128)S(1)}, f32[65,256]{1,0:T(8,128)}, u32[]{:S(2)}) copy-start(f32[65,256]{1,0:T(8,128)} %custom-call) | copy-start | bytes 199684
Sparse Core Ops, SparseCore 0:
  197.5 65.8 reduce-scatter.3
where the time goes:
time: 348 us; the launch traced here: 343 us
  blocking collectives  106 us (30%)
  waiting for transfers between devices  79.3 us (23%)
  matrix products  66.7 us (19%)
  local copies, waits for them, and re-layouts  51.8 us (15%)
  loops' own time  18.2 us (5%)
  between operations  13.6 us (4%)
  other arithmetic  4.33 us (1%)
  starting transfers between devices  3.65 us (1%)
    psum x1, blocking collectives, local(): summed = lax.psum(partial_value, 'seg')  71.7 us
    unnamed x2, waiting for transfers between devices  66 us
    dot_general x130, matrix products, lag_block(): lax.dot_general(own_block, shifted, (((1,), (1,)), ((), ())), preferred_e...  49.9 us
    psum x1, blocking collectives, local(): energies = lax.psum(stacked, 'seg')  34.1 us
    dot_general x16, matrix products, bin_step(): jnp.dot(score_piece, onehot, preferred_element_type=jnp.float32)  16.8 us
    unnamed x16, local copies, waits for them, and re-layouts  15.2 us
    ppermute x2, waiting for transfers between devices, from_behind(): return lax.ppermute(block, axis, route)  13.3 us
    dynamic_update_slice x20, local copies, waits for them, and re-layouts, round_stack(): lax.scan(lag_block, 0, jnp.arange(lag_count // LAG_GROUP, dtype=jnp.int32))  12.9 us
  transfers between devices with their start and end apart: 3, of which 3 were waited for; matrix products, arithmetic and copies ran while one was open for 1% of the time, Pallas kernels for 0%

commit v1 on v0

v1 whole, which is shorter than its diff:
```python
import functools, math
import jax, jax.numpy as jnp
from jax import lax
from jax.sharding import PartitionSpec as P
from jax.experimental import pallas as pl
from jax.experimental.pallas import tpu as pltpu
NT = (((1,), (1,)), ((), ()))
F32, BF = jnp.float32, jnp.bfloat16
W = 1152

def corr_kernel(slot_ref, a0, a1, a2, b_ref, c_ref, c0_ref, a32, lbuf, bbuf):
    k = pl.program_id(0)
    @pl.when(k == 0)
    def _():
        for s in range(2):
            bp = b_ref[s].astype(F32)
            for p in range(8):
                r = bp if p == 0 else pltpu.roll(bp, 8 * p, 1)
                bbuf[s, 128 * p:128 * p + 128, :] = r.astype(BF)
    for kk, a in enumerate((a0, a1, a2)):
        @pl.when(k == kk)
        def _():
            a32[...] = a[...].astype(F32)
    slot = slot_ref[k]
    def blk(ib, _):
        rows = []
        for ii in range(16):
            x = a32[pl.ds(ib * 16 + ii, 1), :]
            x = jnp.broadcast_to(x, (8, W))
            rows.append(pltpu.roll(x, 24, 1, stride=1, stride_axis=0))
        lbuf[pl.ds(pl.multiple_of(ib * 128, 128), 128), :] = jnp.concatenate(rows, 0).astype(BF)
        return 0
    lax.fori_loop(0, 8, blk, 0)
    a_s = pltpu.roll(a32[...], 32, 1).astype(BF)
    c0_ref[0] = lax.dot_general(a_s, b_ref[slot], NT, preferred_element_type=F32)
    for mc in range(4):
        c_ref[0, 256 * mc:256 * mc + 256, :] = lax.dot_general(
            lbuf[256 * mc:256 * mc + 256, :], bbuf[slot], NT, preferred_element_type=F32)

def corr(slots, a0, a1, a2, b):
    vm = lambda shape: pl.BlockSpec(shape, lambda k, *_: (0,) * len(shape))
    return pl.pallas_call(
        corr_kernel,
        grid_spec=pltpu.PrefetchScalarGridSpec(
            num_scalar_prefetch=1, grid=(3,),
            in_specs=[vm((128, W))] * 3 + [vm((2, 128, W))],
            out_specs=[pl.BlockSpec((1, 1024, 1024), lambda k, *_: (k, 0, 0)),
                       pl.BlockSpec((1, 128, 128), lambda k, *_: (k, 0, 0))],
            scratch_shapes=[pltpu.VMEM((128, W), F32), pltpu.VMEM((1024, W), BF), pltpu.VMEM((2, 1024, W), BF)]),
        out_shape=[jax.ShapeDtypeStruct((3, 1024, 1024), F32), jax.ShapeDtypeStruct((3, 128, 128), F32)],
        compiler_params=pltpu.CompilerParams(vmem_limit_bytes=20 << 20),
        cost_estimate=pl.CostEstimate(flops=3 * 2 * 1024 * 1024 * W, bytes_accessed=13 << 20, transcendentals=0),
        name="lag_products",
    )(slots, a0, a1, a2, b)


def bin_kernel(c_ref, c0_ref, scl_ref, bins_ref, out_ref, s_buf, hi, lo, acc):
    k = pl.program_id(0); g = pl.program_id(1)
    @pl.when((k == 0) & (g == 0))
    def _():
        for t in range(3):
            col = jnp.transpose(jnp.broadcast_to(scl_ref[t:t + 1, :], (128, 128)))
            s_buf[t] = col * scl_ref[3 + t:4 + t, :]
        for t in range(4):
            b = bins_ref[t].astype(F32)
            if t % 2 == 0:
                b = jnp.transpose(b)
            h = jnp.floor(b * 0.5)
            hi[t] = h
            lo[t] = b - 2.0 * h
        acc[...] = jnp.zeros_like(acc)
    iota = lax.broadcasted_iota(jnp.int32, (128, 128), 0).astype(F32).astype(BF)
    sub16 = lax.broadcasted_iota(jnp.int32, (16, 128), 0)
    def process(t, a):
        for half in range(2):
            ohs, ws = [], []
            for ii in range(8 * half, 8 * half + 8):
                i = g * 16 + ii
                ct = c_ref[0, 8 * ii:8 * ii + 8, :]
                srow = s_buf[k, pl.ds(i, 1), :]
                z = jnp.concatenate([ct[:, 128 * p:128 * p + 128] for p in range(8)], 0) * srow
                z = z.astype(BF)
                lrow = jnp.broadcast_to(lo[t, pl.ds(i, 1), :], (64, 128)).astype(BF)
                zero = jnp.zeros((64, 128), BF)
                m = lrow == jnp.ones((64, 128), BF)
                z1 = jnp.where(m, z, zero)
                z0 = jnp.where(m, zero, z)
                x0 = c0_ref[0, pl.ds(i, 1), :] * srow
                l1 = lo[t, pl.ds(i, 1), :]
                ex = jnp.where(sub16 == 0, x0 * (1.0 - l1), jnp.where(sub16 == 1, x0 * l1, 0.0)).astype(BF)
                ws.append(jnp.concatenate([z0, z1, ex], 0))
                hrow = jnp.broadcast_to(hi[t, pl.ds(i, 1), :], (128, 128)).astype(BF)
                ohs.append(jnp.where(hrow == iota, jnp.ones((128, 128), BF), jnp.zeros((128, 128), BF)))
            acc[a] += lax.dot_general(jnp.concatenate(ohs, 1), jnp.concatenate(ws, 1), NT, preferred_element_type=F32)
    @pl.when(k == 0)
    def _():
        process(0, 0)
        process(1, 1)
    @pl.when(k == 1)
    def _():
        process(2, 0)
    @pl.when(k == 2)
    def _():
        process(3, 1)
    @pl.when((k == 2) & (g == 7))
    def _():
        c = lax.broadcasted_iota(jnp.int32, (144, 256), 0)
        o = lax.broadcasted_iota(jnp.int32, (144, 256), 1)
        r = c & 63
        m = jnp.where(c < 128, (r >> 3) * 8 + 8 - (r & 7), 0)
        lob = jnp.where(c < 128, c >> 6, c & 1)
        ok = c < 130
        out = jnp.zeros((128, 256), F32)
        for a in range(2):
            l = m if a == 0 else 64 - m
            perm = jnp.where(ok & (o == lob * 128 + l), 1.0, 0.0)
            out = out + lax.dot_general(acc[a], perm, (((1,), (0,)), ((), ())), precision=lax.Precision.HIGHEST, preferred_element_type=F32)
        out_ref[...] = out

def binning(c, c0, scl, bins):
    full = lambda shape: pl.BlockSpec(shape, lambda k, g: (0,) * len(shape))
    return pl.pallas_call(
        bin_kernel, grid=(3, 8),
        in_specs=[pl.BlockSpec((1, 128, 1024), lambda k, g: (k, g, 0)),
                  pl.BlockSpec((1, 128, 128), lambda k, g: (k, 0, 0)),
                  full((8, 128)), full((4, 128, 128))],
        out_specs=full((128, 256)),
        out_shape=jax.ShapeDtypeStruct((128, 256), F32),
        scratch_shapes=[pltpu.VMEM((3, 128, 128), F32), pltpu.VMEM((4, 128, 128), F32), pltpu.VMEM((4, 128, 128), F32),
                        pltpu.VMEM((2, 128, 144), F32)],
        compiler_params=pltpu.CompilerParams(vmem_limit_bytes=20 << 20),
        cost_estimate=pl.CostEstimate(flops=4 * 2 * 128 * 144 * 16384, bytes_accessed=13 << 20, transcendentals=0),
        name="binning",
    )(c, c0, scl, bins)


MAX_LAG = 32
NB = 256
ROUNDS = 2
EPSILON = 1e-06


def exchange(block, source):
    n = lax.axis_size("chan")
    return lax.ppermute(block, "chan", [(source(i), i) for i in range(n)])


def share(block, axis):
    n = lax.axis_size(axis)
    copies = jnp.broadcast_to(block[None], (n,) + block.shape)
    return lax.all_to_all(copies, axis, 0, 0, tiled=True)


def local(traces, pair_bins):
    channels, seg_length = traces.shape
    half_length = seg_length // 2
    total_time = seg_length * lax.axis_size("seg")
    chan_count = lax.axis_size("chan")
    index = lax.axis_index("chan")
    half = index // 8
    first = (index % 8) == 0
    last = (index % 8) == 7
    halves = (traces[:, :half_length], traces[:, half_length:])
    lane = lax.broadcasted_iota(jnp.int32, (channels, 128), 1)
    none = jnp.zeros((channels, 128), traces.dtype)
    halo_low = jnp.where(lane < MAX_LAG, traces[:, half_length:half_length + 128], none)
    halo_high = jnp.where(lane >= 128 - MAX_LAG, traces[:, half_length - 128:half_length], none)
    upper = half == 1
    mine = jnp.where(upper, halves[1], halves[0])
    other = jnp.where(upper, halves[0], halves[1])
    stream_mine, stream_other = jnp.where(upper, none, halo_low), jnp.where(upper, halo_low, none)
    held_mine, held_other = jnp.where(upper, halo_high, none), jnp.where(upper, none, halo_high)
    stream = jnp.concatenate([mine, stream_mine], 1)
    bins = pair_bins.astype(jnp.bfloat16)
    with jax.named_scope("send_blocks"):
        far = exchange(jnp.concatenate([other, held_other, bins[0], bins[1]], 1), lambda i: i ^ 8)
        lower_block = exchange(stream, lambda i: (i & 8) | ((i - 1) & 7))
        upper_payload = jnp.concatenate(
            [jnp.where(first, other, mine), jnp.where(first, stream_other, stream_mine), bins[1]], 1)
        upper_block = exchange(upper_payload, lambda i: (i & 8) | ((i + 1) & 7))
    squares = jnp.sum(jnp.square(traces.astype(jnp.float32)), axis=1)
    with jax.named_scope("energies"):
        energy = jnp.sum(share(squares[None, :], "seg"), axis=0)
        own_scale = lax.rsqrt(energy / total_time + EPSILON)
    with jax.named_scope("send_scales"):
        far_scale = exchange(own_scale, lambda i: i ^ 8)
        lower_scale = exchange(own_scale, lambda i: (i & 8) | ((i - 1) & 7))
        upper_scale = exchange(own_scale, lambda i: (i & 8) | ((i + 1) & 7))
    far_block = far[:, :W]
    far_bins0, far_bins1 = far[:, W:W + 128], far[:, W + 128:]
    special = jnp.concatenate([jnp.where(last, other, mine), jnp.where(last, held_other, held_mine)], 1)
    slots = jnp.stack([jnp.int32(0), first.astype(jnp.int32), last.astype(jnp.int32)])
    products, first_lag = corr(slots, stream, lower_block, upper_block[:, :W], jnp.stack([far_block, special]))
    time_scale = 1.0 / math.sqrt(total_time)
    scales = jnp.concatenate([
        own_scale, lower_scale, upper_scale,
        far_scale * time_scale,
        jnp.where(first, own_scale, far_scale) * time_scale,
        jnp.where(last, own_scale, far_scale) * time_scale,
        jnp.zeros((2, channels), jnp.float32)], 0)
    bin_sets = jnp.stack([far_bins0, bins[0], jnp.where(first, bins[1], far_bins1), upper_block[:, W:]])
    partial_stack = binning(products, first_lag, scales, bin_sets)
    with jax.named_scope("reduce_bins"):
        slots_out = partial_stack.reshape(chan_count, NB // chan_count // 2, 256)
        owned = jnp.sum(lax.all_to_all(slots_out, "chan", 0, 0, tiled=True), axis=0)
        owned = jnp.sum(share(owned, "seg"), axis=0)
    pair_total = ROUNDS * chan_count * channels * channels // NB
    owned = owned.reshape(-1, 2, 128)[:, :, :2 * MAX_LAG + 1] * (1.0 / math.sqrt(pair_total))
    return jnp.transpose(owned, (2, 0, 1)).reshape(2 * MAX_LAG + 1, -1)


def solution(mesh):
    in_specs = (P("chan", "seg"), P(None, "chan", None))
    out_specs = P(None, "chan")
    return jax.shard_map(local, mesh=mesh, in_specs=in_specs, out_specs=out_specs, check_vma=False)
```

time: 348 us -> 90.8 us (0.26); the launches traced: 343 us -> 90.4 us
  blocking collectives: 106 us -> 31.5 us
  waiting for transfers between devices: 79.3 us -> 8.9 us
  matrix products: 66.7 us -> 0 us
  local copies, waits for them, and re-layouts: 51.8 us -> 1.31 us
  Pallas kernels: 0 us -> 25.7 us
  loops' own time: 18.2 us -> 0 us
  starting transfers between devices: 3.65 us -> 18.4 us
  between operations: 13.6 us -> 0.2 us
    psum x2 -> x0, blocking collectives: 106 us -> none  [the longest x1 71.7 us: local(): summed = lax.psum(partial_value, 'seg')]
    dot_general x146 -> x0, matrix products: 66.7 us -> none  [the longest x130 49.9 us: lag_block(): lax.dot_general(own_block, shifted, (((1,), (1,)), ((), ())), preferred_e...]
    unnamed x2 -> x0, waiting for transfers between devices: 66 us -> none
    all_to_all x0 -> x2, blocking collectives: none -> 31.5 us  [the longest x1 19.1 us: share(): return lax.all_to_all(copies, axis, 0, 0, tiled=True)]
    pallas_call x0 -> x2, Pallas kernels: none -> 25.7 us  [the longest x1 14.7 us: corr(): pl.pallas_call(corr_kernel, grid_spec=pltpu.PrefetchScalarGridSpec(num_sc...]
    another operation x4 -> x0, loops' own time: 18.2 us -> none  [the longest x2 11.2 us: round_stack(): lax.scan(bin_step, running, jnp.arange(channels // row_block, dtype=jnp.i...]
    dynamic_slice x42 -> x0, local copies, waits for them, and re-layouts: 16.6 us -> none  [the longest x16 10.4 us: round_stack(): lax.scan(bin_step, running, jnp.arange(channels // row_block, dtype=jnp.i...]
    unnamed x16 -> x0, local copies, waits for them, and re-layouts: 15.2 us -> none
  transfers between devices with their start and end apart: 3 -> 7, of which waited for: 3 -> 2; matrix products, arithmetic and copies ran while one was open for 1% -> 4% of each run, Pallas kernels for 0% -> 0%
where the time goes in v1:
time: 90.8 us; the launch traced here: 90.4 us
  blocking collectives  31.5 us (35%)
  Pallas kernels  25.7 us (28%)
  starting transfers between devices  18.4 us (20%)
  waiting for transfers between devices  8.9 us (10%)
  other arithmetic  4.41 us (5%)
  local copies, waits for them, and re-layouts  1.31 us (1%)
    all_to_all x1, blocking collectives, share(): return lax.all_to_all(copies, axis, 0, 0, tiled=True)  19.1 us
    pallas_call x1, Pallas kernels, corr(): pl.pallas_call(corr_kernel, grid_spec=pltpu.PrefetchScalarGridSpec(num_sc...  14.7 us
    all_to_all x1, blocking collectives, local(): owned = jnp.sum(lax.all_to_all(slots_out, 'chan', 0, 0, tiled=True), axis=0)  12.4 us
    pallas_call x1, Pallas kernels, binning(): pl.pallas_call(bin_kernel, grid=(3, 8), in_specs=[pl.BlockSpec((1, 128, 1...  11.1 us
    ppermute x6, starting transfers between devices, exchange(): return lax.ppermute(block, 'chan', [(source(i), i) for i in range(n)])  9.95 us
    ppermute x6, waiting for transfers between devices, exchange(): return lax.ppermute(block, 'chan', [(source(i), i) for i in range(n)])  8.89 us
    all_to_all x1, starting transfers between devices, share(): return lax.all_to_all(copies, axis, 0, 0, tiled=True)  8.45 us
  transfers between devices with their start and end apart: 7, of which 2 were waited for; matrix products, arithmetic and copies ran while one was open for 4% of the time, Pallas kernels for 0%

profile of v1, /device:TPU:1, one launch (start us, length us, event | category | flops | bytes accessed | tf_op | source)
XLA Modules:
  0.0 90.4 jit_solution(5771391206533760890)
XLA Ops:
  0.0 1.2 %multiply_reduce_fusion = f32[128]{0:T(128)S(1)} fusion(bf16[128,2048]{1,0:T(8,128)(2,1)} %param.2), kind=kLoop, calls=%fused_computation | loop fusion | flops 786304 | bytes 524800 | tf_op jit(solution)/shard_map/reduce_sum | solution.py:181
  1.2 0.6 broadcast_in_dim.9
  1.8 8.4 %all-to-all-start = ((f32[16,1,128]{2,1,0:T(1,128)}), f32[16,1,128]{2,1,0:T(1,128)S(1)}, u32[]{:S(2)}, u32[]{:S(2)}) async-start(f32[16,1,128]{2,1,0:T(1,128)} %broadcast_in_dim.9), calls=%async_computation | async-start | bytes 16384 | tf_op jit(solution)/shard_map/energies/all_to_all | solution.py:151
  10.3 1.1 %broadcast_select_fusion = (bf16[128,1024]{1,0:T(8,128)(2,1)S(1)}, bf16[128,1024]{1,0:T(8,128)(2,1)S(1)}, bf16[128,1024]{1,0:T(8,128)(2,1)S(1)}) fusion(pred[]{:T(512)} %eq.13, bf16[128,2048]{1,0:T(8,128)(2,1)} %param.2, pred[]{:T(512)S(6)} %eq.14), kind=kLoop, calls=%fused_computation.7 | loop fusion | flops 393216 | bytes 1310722 | tf_op jit(solution)/shard_map/jit(_where)/select_n | solution.py:191
  11.4 0.8 broadcast_select_fusion.4
  12.2 1.7 %collective-permute-start = (bf16[128,1152]{1,0:T(8,128)(2,1)S(1)}, bf16[128,1152]{1,0:T(8,128)(2,1)S(1)}, u32[]{:S(2)}, u32[]{:S(2)}) collective-permute-start(bf16[128,1152]{1,0:T(8,128)(2,1)S(1)} %pad_maximum_fusion.3.a0), channel_id=1, source_target_pairs={{112,0},{0,16},{16,32},{32,48},{48,64},{64,80},{80,96},{96,112},{2... | collective-permute-start | bytes 884744 | tf_op jit(solution)/shard_map/send_blocks/ppermute | solution.py:145
  13.9 0.9 %convert_element_type.8 = bf16[2,128,128]{2,1,0:T(8,128)(2,1)S(1)} convert(s32[2,128,128]{2,1,0:T(8,128)} %param.3) | non-fusion elementwise | flops 32768 | bytes 196608 | tf_op jit(solution)/shard_map/convert_element_type | solution.py:174
  15.0 4.0 %collective-permute-start.1 = (bf16[128,1280]{1,0:T(8,128)(2,1)S(1)}, bf16[128,1280]{1,0:T(8,128)(2,1)S(1)}, u32[]{:S(2)}, u32[]{:S(2)}) collective-permute-start(bf16[128,1280]{1,0:T(8,128)(2,1)S(1)} %pad_maximum_fusion.2), channel_id=1, source_target_pairs={{16,0},{32,16},{48,32},{64,48},{80,64},{96,80},{112,96},{0,112},{1... | collective-permute-start | bytes 983048 | tf_op jit(solution)/shard_map/send_blocks/ppermute | solution.py:145
  19.0 0.5 collective-permute-start.2
  19.5 0.0 all-to-all-done
  19.6 1.2 %collective-permute-start.5 = (f32[1,128]{1,0:T(1,128)S(1)}, f32[1,128]{1,0:T(1,128)S(1)}, u32[]{:S(2)}, u32[]{:S(2)}) collective-permute-start(f32[1,128]{1,0:T(1,128)S(1)} %rsqrt_bitcast_fusion), channel_id=1, source_target_pairs={{128,0},{144,16},{160,32},{176,48},{192,64},{208,80},{224,96},{240... | collective-permute-start | bytes 1544 | tf_op jit(solution)/shard_map/send_scales/ppermute | solution.py:145
  20.7 0.1 add_convert_fusion.slot_ref
  20.8 2.6 %collective-permute-start.4 = (f32[1,128]{1,0:T(1,128)S(1)}, f32[1,128]{1,0:T(1,128)S(1)}, u32[]{:S(2)}, u32[]{:S(2)}) collective-permute-start(f32[1,128]{1,0:T(1,128)S(1)} %rsqrt_bitcast_fusion), channel_id=1, source_target_pairs={{16,0},{32,16},{48,32},{64,48},{80,64},{96,80},{112,96},{0,112},{1... | collective-permute-start | bytes 1544 | tf_op jit(solution)/shard_map/send_scales/ppermute | solution.py:145
  23.4 5.3 %collective-permute-done.5 = f32[1,128]{1,0:T(1,128)S(1)} collective-permute-done((f32[1,128]{1,0:T(1,128)S(1)}, f32[1,128]{1,0:T(1,128)S(1)}, u32[]{:S(2)}, u32[]{:S(2)}) %collective-permute-start.5) | collective-permute-done | bytes 544 | tf_op jit(solution)/shard_map/send_scales/ppermute | solution.py:145
  28.7 0.0 collective-permute-start.3
  28.7 0.0 collective-permute-done.4
  28.7 3.6 %collective-permute-done.3 = f32[1,128]{1,0:T(1,128)S(1)} collective-permute-done((f32[1,128]{1,0:T(1,128)S(1)}, f32[1,128]{1,0:T(1,128)S(1)}, u32[]{:S(2)}, u32[]{:S(2)}) %collective-permute-start.3) | collective-permute-done | bytes 544 | tf_op jit(solution)/shard_map/send_scales/ppermute | solution.py:145
  32.3 0.0 collective-permute-done.1
  32.4 0.0 collective-permute-done.2
  32.4 0.1 pad_maximum_fusion.b_ref
  32.5 0.0 collective-permute-done.a1
  32.5 14.7 %lag_products.1 = (f32[3,1024,1024]{2,1,0:T(8,128)S(1)}, f32[3,128,128]{2,1,0:T(8,128)S(1)}) custom-call(s32[3]{0:T(128)S(1)} %add_convert_fusion.slot_ref, bf16[128,1152]{1,0:T(8,128)(2,1)S(1)} %pad_maximum_fusion.3.a0, bf16[128,1152]{1,0:T(8,128)(2,1)S(1)} %collective-permute-done.a1, bf16[128,1152]{1,0:T(8,128)(2,1)S(1)} %slice.52.a2, ...), custom_call_target="tpu_custom_call" | custom-call | flops 7247757312 | bytes 13631488 | tf_op jit(solution)/shard_map/lag_products/pallas_call | solution.py:42
  47.2 11.1 %binning.1 = f32[128,256]{1,0:T(8,128)S(1)} custom-call(f32[3,1024,1024]{2,1,0:T(8,128)S(1)} %get-tuple-element.7.c_ref, f32[3,128,128]{2,1,0:T(8,128)S(1)} %get-tuple-element.8.c0_ref, f32[8,128]{1,0:T(8,128)S(1)} %concatenate.19.scl_ref, bf16[4,128,128]{2,1,0:T(8,128)(2,1)S(1)} %pad_maximum_fusion.4.bins_ref), custom_call_target="tpu_custom_call" | custom-call | flops 2415919104 | bytes 13631488 | tf_op jit(solution)/shard_map/binning/pallas_call | solution.py:122
  58.2 12.4 %all_to_all.15 = f32[16,8,256]{2,1,0:T(8,128)S(1)} all-to-all(f32[16,8,256]{2,1,0:T(8,128)S(1)} %bitcast.30), channel_id=1, replica_groups=mesh['chan'=16,'seg'=16] {'chan'}, dimensions={0} | all-to-all | bytes 262144 | tf_op jit(solution)/shard_map/reduce_bins/all_to_all | solution.py:205
  70.7 19.1 %all_to_all.16 = f32[16,8,256]{2,1,0:T(8,128)S(1)} all-to-all(f32[16,8,256]{2,1,0:T(8,128)S(1)} %broadcast_in_dim.21), channel_id=1, replica_groups=mesh['chan'=16,'seg'=16] {'seg'}, dimensions={0} | all-to-all | bytes 262144 | tf_op jit(solution)/shard_map/reduce_bins/all_to_all | solution.py:151
  89.8 0.6 copy.5
  (21 shorter events, 0.4 us)
Async XLA Ops:
  1.8 17.7 %all-to-all-start = ((f32[16,1,128]{2,1,0:T(1,128)}), f32[16,1,128]{2,1,0:T(1,128)S(1)}, u32[]{:S(2)}, u32[]{:S(2)}) async-start(f32[16,1,128]{2,1,0:T(1,128)} %broadcast_in_dim.9), calls=%async_computation | async-start | bytes 16384 | tf_op jit(solution)/shard_map/energies/all_to_all | solution.py:151
  12.2 20.3 %collective-permute-start = (bf16[128,1152]{1,0:T(8,128)(2,1)S(1)}, bf16[128,1152]{1,0:T(8,128)(2,1)S(1)}, u32[]{:S(2)}, u32[]{:S(2)}) collective-permute-start(bf16[128,1152]{1,0:T(8,128)(2,1)S(1)} %pad_maximum_fusion.3.a0), channel_id=1, source_target_pairs={{112,0},{0,16},{16,32},{32,48},{48,64},{64,80},{80,96},{96,112},{2... | collective-permute-start | bytes 884744 | tf_op jit(solution)/shard_map/send_blocks/ppermute | solution.py:145
  15.0 17.3 %collective-permute-start.1 = (bf16[128,1280]{1,0:T(8,128)(2,1)S(1)}, bf16[128,1280]{1,0:T(8,128)(2,1)S(1)}, u32[]{:S(2)}, u32[]{:S(2)}) collective-permute-start(bf16[128,1280]{1,0:T(8,128)(2,1)S(1)} %pad_maximum_fusion.2), channel_id=1, source_target_pairs={{16,0},{32,16},{48,32},{64,48},{80,64},{96,80},{112,96},{0,112},{1... | collective-permute-start | bytes 983048 | tf_op jit(solution)/shard_map/send_blocks/ppermute | solution.py:145
  19.0 13.3 %collective-permute-start.2 = (bf16[128,1408]{1,0:T(8,128)(2,1)S(1)}, bf16[128,1408]{1,0:T(8,128)(2,1)S(1)}, u32[]{:S(2)}, u32[]{:S(2)}) collective-permute-start(bf16[128,1408]{1,0:T(8,128)(2,1)S(1)} %pad_maximum_fusion.1), channel_id=1, source_target_pairs={{128,0},{144,16},{160,32},{176,48},{192,64},{208,80},{224,96},{240... | collective-permute-start | bytes 1081352 | tf_op jit(solution)/shard_map/send_blocks/ppermute | solution.py:145
  19.6 9.1 %collective-permute-start.5 = (f32[1,128]{1,0:T(1,128)S(1)}, f32[1,128]{1,0:T(1,128)S(1)}, u32[]{:S(2)}, u32[]{:S(2)}) collective-permute-start(f32[1,128]{1,0:T(1,128)S(1)} %rsqrt_bitcast_fusion), channel_id=1, source_target_pairs={{128,0},{144,16},{160,32},{176,48},{192,64},{208,80},{224,96},{240... | collective-permute-start | bytes 1544 | tf_op jit(solution)/shard_map/send_scales/ppermute | solution.py:145
  20.8 7.9 %collective-permute-start.4 = (f32[1,128]{1,0:T(1,128)S(1)}, f32[1,128]{1,0:T(1,128)S(1)}, u32[]{:S(2)}, u32[]{:S(2)}) collective-permute-start(f32[1,128]{1,0:T(1,128)S(1)} %rsqrt_bitcast_fusion), channel_id=1, source_target_pairs={{16,0},{32,16},{48,32},{64,48},{80,64},{96,80},{112,96},{0,112},{1... | collective-permute-start | bytes 1544 | tf_op jit(solution)/shard_map/send_scales/ppermute | solution.py:145
  28.7 3.6 %collective-permute-start.3 = (f32[1,128]{1,0:T(1,128)S(1)}, f32[1,128]{1,0:T(1,128)S(1)}, u32[]{:S(2)}, u32[]{:S(2)}) collective-permute-start(f32[1,128]{1,0:T(1,128)S(1)} %rsqrt_bitcast_fusion), channel_id=1, source_target_pairs={{112,0},{0,16},{16,32},{32,48},{48,64},{64,80},{80,96},{96,112},{2... | collective-permute-start | bytes 1544 | tf_op jit(solution)/shard_map/send_scales/ppermute | solution.py:145

commit v2 on v0

v2 whole, which is shorter than its diff:
```python
import functools
import math

import jax
import jax.numpy as jnp
from jax import lax
from jax.experimental import pallas as pl
from jax.experimental.pallas import tpu as pltpu
from jax.sharding import PartitionSpec as P

NT = (((1,), (1,)), ((), ()))
NN = (((1,), (0,)), ((), ()))
F32, BF = jnp.float32, jnp.bfloat16
W = 1152
CB = 128
VMEM = pl.BlockSpec(memory_space=pltpu.VMEM)
SMEM = pl.BlockSpec(memory_space=pltpu.SMEM)


def lag_rows(ref, start, count):
    rows = []
    for ii in range(count):
        x = jnp.broadcast_to(ref[pl.ds(start + ii, 1), :], (8, W))
        rows.append(pltpu.roll(x, 24, 1, stride=1, stride_axis=0))
    return jnp.concatenate(rows, 0).astype(BF)


def shift_rows(block, out_ref):
    for p in range(8):
        out_ref[CB * p:CB * p + CB, :] = block if p == 0 else pltpu.roll(block, 8 * p, 1)


GROUP = 8
CHUNK = 256


def fused_kernel(time_scale, flags, scale_ref, bins_ref, stream, lower, upper, far, special, out_ref,
                 wide, lags, shifted, c_ref, c0_ref, pair_scale, hi, lo, acc0, acc1):
    shift_rows(far[:, :W], shifted.at[0])
    shift_rows(special[...], shifted.at[1])
    wide[0] = stream[...].astype(F32)
    wide[1] = lower[...].astype(F32)
    wide[2] = upper[:, :W].astype(F32)
    first, last = flags[1] == 1, flags[2] == 1
    own, far_scale = scale_ref[0:1, :], scale_ref[1:2, :]
    held = (far_scale, jnp.where(first, own, far_scale), jnp.where(last, own, far_scale))
    for t, streamed in enumerate((own, scale_ref[2:3, :], scale_ref[3:4, :])):
        column = jnp.transpose(jnp.broadcast_to(streamed, (CB, CB)))
        pair_scale[t] = column * (held[t] * time_scale)
    sets = (far[:, W:W + CB].astype(F32), bins_ref[0].astype(F32),
            jnp.where(first, bins_ref[1].astype(F32), far[:, W + CB:].astype(F32)), upper[:, W:].astype(F32))
    for t, b in enumerate(sets):
        if t % 2 == 0:
            b = jnp.transpose(b)
        h = jnp.floor(b * 0.5)
        hi[t] = h
        lo[t] = b - 2.0 * h
    acc0[...] = jnp.zeros_like(acc0)
    acc1[...] = jnp.zeros_like(acc1)
    iota = lax.broadcasted_iota(jnp.int32, (CB, CB), 0).astype(F32).astype(BF)
    one, zero = jnp.ones((CB, CB), BF), jnp.zeros((CB, CB), BF)
    sub = lax.broadcasted_iota(jnp.int32, (32, CB), 0) & 7
    slots = (0, flags[1], flags[2])
    for k, block in enumerate((stream[...], lower[...], upper[:, :W])):
        c0_ref[k] = lax.dot_general(pltpu.roll(block, 32, 1), shifted[slots[k], :CB, :], NT, preferred_element_type=F32)

    def zscore(k, i):
        rows = c_ref[k, 8 * i:8 * i + 8, :]
        z = jnp.concatenate([rows[:, CB * p:CB * p + CB] for p in range(8)], 0)
        return (z * pair_scale[k, i:i + 1, :]).astype(BF)

    def low(t, i):
        return jnp.broadcast_to(lo[t, i:i + 1, :], (64, CB)).astype(BF)

    def onehot(t, i):
        return jnp.where(jnp.broadcast_to(hi[t, i:i + 1, :], (CB, CB)).astype(BF) == iota, one, zero)

    def bin_group(base):
        rows = pl.ds(base, GROUP)
        x = [c0_ref[k, rows, :] * pair_scale[k, rows, :] for k in range(3)]
        low8 = [lo[t, rows, :] for t in range(4)]
        extra0 = jnp.concatenate([x[0], x[0] * low8[0], x[0] * low8[1], jnp.zeros_like(x[0])], 0)
        extra1 = jnp.concatenate([x[1], x[1] * low8[2], x[2], x[2] * low8[3]], 0)
        left0, left1, right0, right1 = [], [], [], []
        for ii in range(GROUP):
            i = base + ii
            e0 = jnp.where(sub == ii, extra0, 0.0).astype(BF)
            e1 = jnp.where(sub == ii, extra1, 0.0).astype(BF)
            z = [zscore(k, i) for k in range(3)]
            left0.append(jnp.concatenate([z[0], z[0] * low(0, i), z[0] * low(1, i), e0], 0))
            left1.append(jnp.concatenate([z[1], z[1] * low(2, i), z[2], z[2] * low(3, i), e1], 0))
            right0.append(jnp.concatenate([onehot(0, i), onehot(1, i)], 0))
            right1.append(jnp.concatenate([onehot(2, i), onehot(3, i)], 0))
        cat = lambda blocks: jnp.concatenate(blocks, 1)
        acc0[...] += lax.dot_general(cat(left0), cat(right0), NT, preferred_element_type=F32)
        acc1[...] += lax.dot_general(cat(left1), cat(right1), NT, preferred_element_type=F32)

    def bin_chunk(m):
        for g in range(CHUNK // 8 // GROUP):
            bin_group(m * (CHUNK // 8) + g * GROUP)

    for m in range(1024 // CHUNK):
        rows = slice(m * CHUNK, (m + 1) * CHUNK)
        for k in range(3):
            lags[k, rows, :] = lag_rows(wide.at[k], m * CHUNK // 8, CHUNK // 8)
            c_ref[k, rows, :] = lax.dot_general(lags[k, rows, :], shifted[slots[k]], NT, preferred_element_type=F32)
        if m > 0:
            bin_chunk(m - 1)
    bin_chunk(1024 // CHUNK - 1)

    total = lambda v: jnp.sum(v, axis=0, keepdims=True)
    forward = [acc0[0:64, :CB] + acc1[0:64, :CB], acc0[64:128, :CB] + acc1[64:128, :CB]]
    reverse = [acc0[0:64, CB:] + acc1[128:192, CB:], acc0[128:192, CB:] + acc1[192:256, CB:]]
    forward0 = [total(acc0[192:200, :CB]) + total(acc1[256:264, :CB]), total(acc0[200:208, :CB]) + total(acc1[264:272, :CB])]
    reverse0 = [total(acc0[192:200, CB:]) + total(acc1[272:280, CB:]), total(acc0[208:216, CB:]) + total(acc1[280:288, CB:])]
    lag = lax.broadcasted_iota(jnp.int32, (CB, 64), 0)
    r = lax.broadcasted_iota(jnp.int32, (CB, 64), 1)
    m = (r >> 3) * 8 + 8 - (r & 7)
    to_forward = jnp.where(lag == m, 1.0, 0.0)
    to_reverse = jnp.where(lag == 64 - m, 1.0, 0.0)
    lag_row = lax.broadcasted_iota(jnp.int32, (CB, CB), 0)
    parts = []
    for q in range(2):
        exact = lambda s, v: lax.dot_general(s, v, NN, precision=lax.Precision.HIGHEST, preferred_element_type=F32)
        part = exact(to_forward, forward[q]) + exact(to_reverse, reverse[q])
        part = part + jnp.where(lag_row == 0, forward0[q], 0.0) + jnp.where(lag_row == 64, reverse0[q], 0.0)
        parts.append(part)
    out_ref[:, :CB] = jnp.transpose(parts[0] - parts[1])
    out_ref[:, CB:] = jnp.transpose(parts[1])


def fused(flags, scales, bins, stream, lower, upper, far, special, time_scale):
    return pl.pallas_call(
        functools.partial(fused_kernel, time_scale),
        in_specs=[SMEM] + [VMEM] * 7,
        out_specs=VMEM,
        out_shape=jax.ShapeDtypeStruct((CB, 2 * CB), F32),
        scratch_shapes=[pltpu.VMEM((3, CB, W), F32), pltpu.VMEM((3, 1024, W), BF),
                        pltpu.VMEM((2, 1024, W), BF), pltpu.VMEM((3, 1024, 1024), F32), pltpu.VMEM((3, CB, CB), F32),
                        pltpu.VMEM((3, CB, CB), F32), pltpu.VMEM((4, CB, CB), F32), pltpu.VMEM((4, CB, CB), F32),
                        pltpu.VMEM((224, 2 * CB), F32), pltpu.VMEM((288, 2 * CB), F32)],
        compiler_params=pltpu.CompilerParams(vmem_limit_bytes=36 << 20),
        cost_estimate=pl.CostEstimate(flops=4 * 2 * 1024 * 1024 * W, bytes_accessed=6 << 20, transcendentals=0),
        name="lags_and_bins",
    )(flags, scales, bins, stream, lower, upper, far, special)


MAX_LAG = 32
NB = 256
ROUNDS = 2
EPSILON = 1e-06
HALF = 1024


def payload_kernel(flags, squares, traces, bins, stream_ref, far_ref, upper_ref, special_ref, edge, bins_v, sems):
    high, first, last = (flags[i] == 1 for i in range(3))
    mine = pl.multiple_of(jnp.where(high, HALF, 0), HALF)
    other = pl.multiple_of(HALF - mine, HALF)
    upper_start = pl.multiple_of(jnp.where(first, other, mine), HALF)
    special_start = pl.multiple_of(jnp.where(last, other, mine), HALF)
    part = lambda start: traces.at[:, pl.ds(start, HALF)]
    main = pl.ds(0, HALF)
    copies = [pltpu.make_async_copy(traces.at[:, pl.ds(HALF - CB, 2 * CB)], edge, sems.at[0]),
              pltpu.make_async_copy(bins, bins_v, sems.at[1])]
    for n, (start, ref) in enumerate(((mine, stream_ref), (other, far_ref), (upper_start, upper_ref), (special_start, special_ref))):
        copies.append(pltpu.make_async_copy(part(start), ref.at[:, main], sems.at[2 + n]))
    for copy in copies:
        copy.start()
    lane = lax.broadcasted_iota(jnp.int32, (CB, CB), 1)
    none = jnp.zeros((CB, CB), F32)
    copies[0].wait()
    halo_low = jnp.where(lane < MAX_LAG, edge[:, CB:].astype(F32), none)
    halo_high = jnp.where(lane >= CB - MAX_LAG, edge[:, :CB].astype(F32), none)
    keep_low = jnp.where(high, 0.0, 1.0)
    keep_high = 1.0 - keep_low
    stream_ref[:, HALF:] = (halo_low * keep_low).astype(BF)
    upper_ref[:, HALF:W] = (halo_low * jnp.where(first, keep_high, keep_low)).astype(BF)
    far_ref[:, HALF:W] = (halo_high * keep_low).astype(BF)
    special_ref[:, HALF:] = (halo_high * jnp.where(last, keep_low, keep_high)).astype(BF)
    copies[1].wait()
    far_ref[:, W:W + CB] = bins_v[0].astype(F32).astype(BF)
    far_ref[:, W + CB:] = bins_v[1].astype(F32).astype(BF)
    upper_ref[:, W:] = bins_v[1].astype(F32).astype(BF)
    for copy in copies[2:]:
        copy.wait()


def payloads(flags, squares, traces, bins):
    return pl.pallas_call(
        payload_kernel,
        in_specs=[SMEM, VMEM, pl.BlockSpec(memory_space=pl.ANY), pl.BlockSpec(memory_space=pl.ANY)],
        out_specs=[VMEM] * 4,
        out_shape=[jax.ShapeDtypeStruct((CB, width), BF) for width in (W, W + 2 * CB, W + CB, W)],
        scratch_shapes=[pltpu.VMEM((CB, 2 * CB), BF), pltpu.VMEM((2, CB, CB), jnp.int32), pltpu.SemaphoreType.DMA((6,))],
        compiler_params=pltpu.CompilerParams(vmem_limit_bytes=8 << 20),
        cost_estimate=pl.CostEstimate(flops=1 << 18, bytes_accessed=2 << 20, transcendentals=0),
        name="payloads",
    )(flags, squares, traces, bins)


def square_kernel(traces, out_ref):
    total = jnp.zeros((CB, CB), F32)
    for t in range(2 * HALF // CB):
        x = traces[:, CB * t:CB * t + CB].astype(F32)
        total = total + x * x
    out_ref[...] = jnp.sum(jnp.transpose(total), axis=0, keepdims=True)


def square_sums(traces):
    return pl.pallas_call(
        square_kernel,
        in_specs=[VMEM],
        out_specs=VMEM,
        out_shape=jax.ShapeDtypeStruct((1, CB), F32),
        compiler_params=pltpu.CompilerParams(vmem_limit_bytes=4 << 20),
        cost_estimate=pl.CostEstimate(flops=1 << 18, bytes_accessed=1 << 19, transcendentals=0),
        name="square_sums",
    )(traces)


def copies_kernel(*refs):
    rows = jnp.concatenate([ref[...] for ref in refs[:-1]], 0)
    refs[-1][...] = jnp.broadcast_to(rows[None], refs[-1].shape)


def copies_of(rows, count):
    return pl.pallas_call(
        copies_kernel,
        in_specs=[VMEM] * len(rows),
        out_specs=VMEM,
        out_shape=jax.ShapeDtypeStruct((count, len(rows), CB), F32),
        compiler_params=pltpu.CompilerParams(vmem_limit_bytes=2 << 20),
        cost_estimate=pl.CostEstimate(flops=1 << 12, bytes_accessed=1 << 15, transcendentals=0),
        name="square_copies",
    )(*rows)


def inverse_rms_kernel(total_time, gathered, out_ref):
    out_ref[...] = lax.rsqrt(jnp.sum(gathered[...], axis=0) / total_time + EPSILON)


def inverse_rms(gathered, total_time):
    return pl.pallas_call(
        functools.partial(inverse_rms_kernel, total_time),
        in_specs=[VMEM],
        out_specs=VMEM,
        out_shape=jax.ShapeDtypeStruct((4, CB), F32),
        compiler_params=pltpu.CompilerParams(vmem_limit_bytes=2 << 20),
        cost_estimate=pl.CostEstimate(flops=1 << 12, bytes_accessed=1 << 13, transcendentals=0),
        name="inverse_rms",
    )(gathered)


def exchange(block, source):
    n = lax.axis_size("chan")
    return lax.ppermute(block, "chan", [(source(i), i) for i in range(n)])


FAR = lambda i: i ^ 8
LOWER = lambda i: (i & 8) | ((i - 1) & 7)
UPPER = lambda i: (i & 8) | ((i + 1) & 7)


def local(traces, pair_bins):
    total_time = traces.shape[1] * lax.axis_size("seg")
    chan_count, seg_count = lax.axis_size("chan"), lax.axis_size("seg")
    index = lax.axis_index("chan")
    depth = index % 8
    flags = jnp.stack([index // 8, (depth == 0).astype(jnp.int32), (depth == 7).astype(jnp.int32)])
    squares = square_sums(traces)
    stream, far_payload, upper_payload, special = payloads(flags, squares, traces, pair_bins)
    with jax.named_scope("send_squares"):
        rows = [squares] + [exchange(squares, source) for source in (FAR, LOWER, UPPER)]
    rows, stream, far_payload, upper_payload = lax.optimization_barrier((rows, stream, far_payload, upper_payload))
    with jax.named_scope("send_blocks"):
        far = exchange(far_payload, FAR)
        lower = exchange(stream, LOWER)
        upper = exchange(upper_payload, UPPER)
    with jax.named_scope("energies"):
        gathered = lax.all_to_all(copies_of(rows, seg_count), "seg", 0, 0, tiled=True)
        scales = inverse_rms(gathered, total_time)
    partial_stack = fused(flags, scales, pair_bins, stream, lower, upper, far, special,
                          1.0 / math.sqrt(total_time))
    with jax.named_scope("reduce_bins"):
        slots = partial_stack.reshape(chan_count, CB // chan_count, 2 * CB)
        owned = jnp.sum(lax.all_to_all(slots, "chan", 0, 0, tiled=True), axis=0)
        copies = jnp.broadcast_to(owned[None], (seg_count,) + owned.shape)
        owned = jnp.sum(lax.all_to_all(copies, "seg", 0, 0, tiled=True), axis=0)
    pair_total = ROUNDS * chan_count * CB * CB // NB
    owned = owned.reshape(-1, 2, CB)[:, :, :2 * MAX_LAG + 1] * (1.0 / math.sqrt(pair_total))
    return jnp.transpose(owned, (2, 0, 1)).reshape(2 * MAX_LAG + 1, -1)


def solution(mesh):
    in_specs = (P("chan", "seg"), P(None, "chan", None))
    out_specs = P(None, "chan")
    return jax.shard_map(local, mesh=mesh, in_specs=in_specs, out_specs=out_specs, check_vma=False)
```

time: 348 us -> 74.4 us (0.21); the launches traced: 343 us -> 74.2 us
  waiting for transfers between devices: 79.3 us -> 0.02 us
  matrix products: 66.7 us -> 0 us
  blocking collectives: 106 us -> 42.8 us
  local copies, waits for them, and re-layouts: 51.8 us -> 2.57 us
  Pallas kernels: 0 us -> 19 us
  loops' own time: 18.2 us -> 0 us
  between operations: 13.6 us -> 0.11 us
  starting transfers between devices: 3.65 us -> 9.62 us
  other arithmetic: 4.33 us -> 0.12 us
    psum x2 -> x0, blocking collectives: 106 us -> none  [the longest x1 71.7 us: local(): summed = lax.psum(partial_value, 'seg')]
    dot_general x146 -> x0, matrix products: 66.7 us -> none  [the longest x130 49.9 us: lag_block(): lax.dot_general(own_block, shifted, (((1,), (1,)), ((), ())), preferred_e...]
    unnamed x2 -> x0, waiting for transfers between devices: 66 us -> none
    all_to_all x0 -> x3, blocking collectives: none -> 42.8 us  [the longest x1 16.7 us: local(): lax.all_to_all(copies_of(rows, seg_count), 'seg', 0, 0, tiled=True)]
    pallas_call x0 -> x5, Pallas kernels: none -> 19 us  [the longest x1 17.9 us: fused(): pl.pallas_call(functools.partial(fused_kernel, time_scale), in_specs=[SME...]
    another operation x4 -> x0, loops' own time: 18.2 us -> none  [the longest x2 11.2 us: round_stack(): lax.scan(bin_step, running, jnp.arange(channels // row_block, dtype=jnp.i...]
    dynamic_slice x42 -> x0, local copies, waits for them, and re-layouts: 16.6 us -> none  [the longest x16 10.4 us: round_stack(): lax.scan(bin_step, running, jnp.arange(channels // row_block, dtype=jnp.i...]
    ppermute x2 -> x6, waiting for transfers between devices: 13.3 us -> 0.02 us  [exchange(): return lax.ppermute(block, 'chan', [(source(i), i) for i in range(n)])]
  transfers between devices with their start and end apart: 3 -> 6, of which waited for: 3 -> 0; matrix products, arithmetic and copies ran while one was open for 1% -> 0% of each run, Pallas kernels for 0% -> 1%
where the time goes in v2:
time: 74.4 us; the launch traced here: 74.2 us
  blocking collectives  42.8 us (58%)
  Pallas kernels  19 us (26%)
  starting transfers between devices  9.62 us (13%)
  local copies, waits for them, and re-layouts  2.57 us (3%)
    pallas_call x1, Pallas kernels, fused(): pl.pallas_call(functools.partial(fused_kernel, time_scale), in_specs=[SME...  17.9 us
    all_to_all x1, blocking collectives, local(): lax.all_to_all(copies_of(rows, seg_count), 'seg', 0, 0, tiled=True)  16.7 us
    all_to_all x1, blocking collectives, local(): owned = jnp.sum(lax.all_to_all(slots, 'chan', 0, 0, tiled=True), axis=0)  13.6 us
    all_to_all x1, blocking collectives, local(): owned = jnp.sum(lax.all_to_all(copies, 'seg', 0, 0, tiled=True), axis=0)  12.5 us
    ppermute x6, starting transfers between devices, exchange(): return lax.ppermute(block, 'chan', [(source(i), i) for i in range(n)])  9.62 us
    unnamed x8, local copies, waits for them, and re-layouts  1.96 us
  transfers between devices with their start and end apart: 6, of which 0 were waited for; matrix products, arithmetic and copies ran while one was open for 0% of the time, Pallas kernels for 1%

profile of v2, /device:TPU:1, one launch (start us, length us, event | category | flops | bytes accessed | tf_op | source)
XLA Modules:
  0.0 74.2 jit_solution(12636519540439527846)
XLA Ops:
  0.0 0.0 copy-start
  0.0 1.0 %copy-done = bf16[128,2048]{1,0:T(8,128)(2,1)S(1)} copy-done((bf16[128,2048]{1,0:T(8,128)(2,1)S(1)}, bf16[128,2048]{1,0:T(8,128)(2,1)}, u32[]{:S(2)}) %copy-start) | copy-done | bytes 524312
  1.0 0.0 copy-start.1
  1.0 0.2 square_sums.1.squares.refs_0_
  1.2 2.2 %collective-permute-start = (f32[1,128]{1,0:T(1,128)S(1)}, f32[1,128]{1,0:T(1,128)S(1)}, u32[]{:S(2)}, u32[]{:S(2)}) collective-permute-start(f32[1,128]{1,0:T(1,128)S(1)} %square_sums.1.squares.refs_0_), channel_id=1, source_target_pairs={{128,0},{144,16},{160,32},{176,48},{192,64},{208,80},{224,96},{240... | collective-permute-start | bytes 1544 | tf_op jit(solution)/shard_map/send_squares/ppermute | solution.py:256
  3.4 1.6 %collective-permute-start.1 = (f32[1,128]{1,0:T(1,128)S(1)}, f32[1,128]{1,0:T(1,128)S(1)}, u32[]{:S(2)}, u32[]{:S(2)}) collective-permute-start(f32[1,128]{1,0:T(1,128)S(1)} %square_sums.1.squares.refs_0_), channel_id=1, source_target_pairs={{112,0},{0,16},{16,32},{32,48},{48,64},{64,80},{80,96},{96,112},{2... | collective-permute-start | bytes 1544 | tf_op jit(solution)/shard_map/send_squares/ppermute | solution.py:256
  5.1 3.9 %collective-permute-start.2 = (f32[1,128]{1,0:T(1,128)S(1)}, f32[1,128]{1,0:T(1,128)S(1)}, u32[]{:S(2)}, u32[]{:S(2)}) collective-permute-start(f32[1,128]{1,0:T(1,128)S(1)} %square_sums.1.squares.refs_0_), channel_id=1, source_target_pairs={{16,0},{32,16},{48,32},{64,48},{80,64},{96,80},{112,96},{0,112},{1... | collective-permute-start | bytes 1544 | tf_op jit(solution)/shard_map/send_squares/ppermute | solution.py:256
  9.0 0.1 pad_add_fusion.flags
  9.1 0.0 copy-done.1
  9.1 0.0 copy-start.2
  9.1 0.9 %copy-done.2 = s32[2,128,128]{2,1,0:T(8,128)S(1)} copy-done((s32[2,128,128]{2,1,0:T(8,128)S(1)}, s32[2,128,128]{2,1,0:T(8,128)}, u32[]{:S(2)}) %copy-start.2) | copy-done | bytes 131096
  10.0 0.9 %payloads.1 = (bf16[128,1152]{1,0:T(8,128)(2,1)S(1)}, bf16[128,1408]{1,0:T(8,128)(2,1)S(1)}, bf16[128,1280]{1,0:T(8,128)(2,1)S(1)}, bf16[128,1152]{1,0:T(8,128)(2,1)S(1)}) custom-call(s32[3]{0:T(128)S(1)} %pad_add_fusion.flags, f32[1,128]{1,0:T(1,128)S(1)} %square_sums.1.squares.refs_0_, bf16[128,2048]{1,0:T(8,128)(2,1)S(1)} %copy-done.1, ...), custom_call_target="tpu_custom_call" | custom-call | flops 262144 | bytes 2097152 | tf_op jit(solution)/shard_map/payloads/pallas_call | solution.py:189
  10.9 0.0 copy-start.3
  10.9 0.0 collective-permute-done.refs_1_
  10.9 0.0 collective-permute-done.1.refs_2_
  10.9 0.0 collective-permute-done.2.refs_3_
  11.0 0.3 collective-permute-start.5
  11.2 1.6 %collective-permute-start.4 = (bf16[128,1280]{1,0:T(8,128)(2,1)S(1)}, bf16[128,1280]{1,0:T(8,128)(2,1)S(1)}, u32[]{:S(2)}, u32[]{:S(2)}) collective-permute-start(bf16[128,1280]{1,0:T(8,128)(2,1)S(1)} %get-tuple-element.24), channel_id=1, source_target_pairs={{16,0},{32,16},{48,32},{64,48},{80,64},{96,80},{112,96},{0,112},{1... | collective-permute-start | bytes 983048 | tf_op jit(solution)/shard_map/send_blocks/ppermute | solution.py:256
  12.8 0.0 collective-permute-start.3
  12.8 16.7 %all_to_all.15.gathered = f32[16,4,128]{2,1,0:T(4,128)S(1)} all-to-all(f32[16,4,128]{2,1,0:T(4,128)S(1)} %square_copies.1), channel_id=1, replica_groups=mesh['chan'=16,'seg'=16] {'seg'}, dimensions={0} | all-to-all | bytes 65536 | tf_op jit(solution)/shard_map/energies/all_to_all | solution.py:280
  29.5 0.0 collective-permute-done.3.lower
  29.5 0.0 collective-permute-done.4.upper
  29.5 0.0 collective-permute-done.5.far
  29.6 0.0 copy-done.3
  29.6 17.9 %lags_and_bins.1 = f32[128,256]{1,0:T(8,128)S(1)} custom-call(s32[3]{0:T(128)S(1)} %pad_add_fusion.flags, f32[4,128]{1,0:T(4,128)S(1)} %inverse_rms.1.scale_ref, s32[2,128,128]{2,1,0:T(8,128)S(1)} %copy-done.3, bf16[128,1152]{1,0:T(8,128)(2,1)S(1)} %get-tuple-element.23.stream, bf16[128,1152]{1,0:T(8,128)(2,1)S(1)} %collective-permute-done.3.lower, ...), custom_call_target="tpu_custom_call" | custom-call | flops 9663676416 | bytes 6291456 | tf_op jit(solution)/shard_map/lags_and_bins/pallas_call | solution.py:133
  47.4 13.6 %all_to_all.16 = f32[16,8,256]{2,1,0:T(8,128)S(1)} all-to-all(f32[16,8,256]{2,1,0:T(8,128)S(1)} %bitcast.8), channel_id=1, replica_groups=mesh['chan'=16,'seg'=16] {'chan'}, dimensions={0} | all-to-all | bytes 262144 | tf_op jit(solution)/shard_map/reduce_bins/all_to_all | solution.py:286
  61.0 12.5 %all_to_all.17 = f32[16,8,256]{2,1,0:T(8,128)S(1)} all-to-all(f32[16,8,256]{2,1,0:T(8,128)S(1)} %broadcast_in_dim.2), channel_id=1, replica_groups=mesh['chan'=16,'seg'=16] {'seg'}, dimensions={0} | all-to-all | bytes 262144 | tf_op jit(solution)/shard_map/reduce_bins/all_to_all | solution.py:288
  73.6 0.6 copy.3
  (6 shorter events, 0.1 us)
Async XLA Ops:
  0.0 1.0 %copy-start = (bf16[128,2048]{1,0:T(8,128)(2,1)S(1)}, bf16[128,2048]{1,0:T(8,128)(2,1)}, u32[]{:S(2)}) copy-start(bf16[128,2048]{1,0:T(8,128)(2,1)} %traces.3) | copy-start | bytes 1572868
  1.0 8.0 %copy-start.1 = (bf16[128,2048]{1,0:T(8,128)(2,1)S(1)}, bf16[128,2048]{1,0:T(8,128)(2,1)}, u32[]{:S(2)}) copy-start(bf16[128,2048]{1,0:T(8,128)(2,1)} %traces.3) | copy-start | bytes 1572868
  1.2 9.7 %collective-permute-start = (f32[1,128]{1,0:T(1,128)S(1)}, f32[1,128]{1,0:T(1,128)S(1)}, u32[]{:S(2)}, u32[]{:S(2)}) collective-permute-start(f32[1,128]{1,0:T(1,128)S(1)} %square_sums.1.squares.refs_0_), channel_id=1, source_target_pairs={{128,0},{144,16},{160,32},{176,48},{192,64},{208,80},{224,96},{240... | collective-permute-start | bytes 1544 | tf_op jit(solution)/shard_map/send_squares/ppermute | solution.py:256
  3.4 7.5 %collective-permute-start.1 = (f32[1,128]{1,0:T(1,128)S(1)}, f32[1,128]{1,0:T(1,128)S(1)}, u32[]{:S(2)}, u32[]{:S(2)}) collective-permute-start(f32[1,128]{1,0:T(1,128)S(1)} %square_sums.1.squares.refs_0_), channel_id=1, source_target_pairs={{112,0},{0,16},{16,32},{32,48},{48,64},{64,80},{80,96},{96,112},{2... | collective-permute-start | bytes 1544 | tf_op jit(solution)/shard_map/send_squares/ppermute | solution.py:256
  5.1 5.9 %collective-permute-start.2 = (f32[1,128]{1,0:T(1,128)S(1)}, f32[1,128]{1,0:T(1,128)S(1)}, u32[]{:S(2)}, u32[]{:S(2)}) collective-permute-start(f32[1,128]{1,0:T(1,128)S(1)} %square_sums.1.squares.refs_0_), channel_id=1, source_target_pairs={{16,0},{32,16},{48,32},{64,48},{80,64},{96,80},{112,96},{0,112},{1... | collective-permute-start | bytes 1544 | tf_op jit(solution)/shard_map/send_squares/ppermute | solution.py:256
  9.1 0.9 %copy-start.2 = (s32[2,128,128]{2,1,0:T(8,128)S(1)}, s32[2,128,128]{2,1,0:T(8,128)}, u32[]{:S(2)}) copy-start(s32[2,128,128]{2,1,0:T(8,128)} %bins_ref.1) | copy-start | bytes 393220
  10.9 18.6 %copy-start.3 = (s32[2,128,128]{2,1,0:T(8,128)S(1)}, s32[2,128,128]{2,1,0:T(8,128)}, u32[]{:S(2)}) copy-start(s32[2,128,128]{2,1,0:T(8,128)} %bins_ref.1) | copy-start | bytes 393220
  11.0 18.6 %collective-permute-start.5 = (bf16[128,1408]{1,0:T(8,128)(2,1)S(1)}, bf16[128,1408]{1,0:T(8,128)(2,1)S(1)}, u32[]{:S(2)}, u32[]{:S(2)}) collective-permute-start(bf16[128,1408]{1,0:T(8,128)(2,1)S(1)} %get-tuple-element.25), channel_id=1, source_target_pairs={{128,0},{144,16},{160,32},{176,48},{192,64},{208,80},{224,96},{240... | collective-permute-start | bytes 1081352 | tf_op jit(solution)/shard_map/send_blocks/ppermute | solution.py:256
  11.2 18.3 %collective-permute-start.4 = (bf16[128,1280]{1,0:T(8,128)(2,1)S(1)}, bf16[128,1280]{1,0:T(8,128)(2,1)S(1)}, u32[]{:S(2)}, u32[]{:S(2)}) collective-permute-start(bf16[128,1280]{1,0:T(8,128)(2,1)S(1)} %get-tuple-element.24), channel_id=1, source_target_pairs={{16,0},{32,16},{48,32},{64,48},{80,64},{96,80},{112,96},{0,112},{1... | collective-permute-start | bytes 983048 | tf_op jit(solution)/shard_map/send_blocks/ppermute | solution.py:256
  12.8 16.7 %collective-permute-start.3 = (bf16[128,1152]{1,0:T(8,128)(2,1)S(1)}, bf16[128,1152]{1,0:T(8,128)(2,1)S(1)}, u32[]{:S(2)}, u32[]{:S(2)}) collective-permute-start(bf16[128,1152]{1,0:T(8,128)(2,1)S(1)} %get-tuple-element.23.stream), channel_id=1, source_target_pairs={{112,0},{0,16},{16,32},{32,48},{48,64},{64,80},{80,96},{96,112},{2... | collective-permute-start | bytes 884744 | tf_op jit(solution)/shard_map/send_blocks/ppermute | solution.py:256

commit v3 on v2

--- a/solution.py
+++ b/solution.py
@@ -31,51 +31,33 @@
 
 
 GROUP = 8
-CHUNK = 256
+STEP = 64
 
 
 def fused_kernel(time_scale, flags, scale_ref, bins_ref, stream, lower, upper, far, special, out_ref,
-                 wide, lags, shifted, c_ref, c0_ref, pair_scale, hi, lo, acc0, acc1):
+                 wide, lags, shifted, c_first, c_ref, c0_ref, pair_scale, hi, lo, acc0, acc1):
     shift_rows(far[:, :W], shifted.at[0])
-    shift_rows(special[...], shifted.at[1])
     wide[0] = stream[...].astype(F32)
     wide[1] = lower[...].astype(F32)
     wide[2] = upper[:, :W].astype(F32)
-    first, last = flags[1] == 1, flags[2] == 1
-    own, far_scale = scale_ref[0:1, :], scale_ref[1:2, :]
-    held = (far_scale, jnp.where(first, own, far_scale), jnp.where(last, own, far_scale))
-    for t, streamed in enumerate((own, scale_ref[2:3, :], scale_ref[3:4, :])):
-        column = jnp.transpose(jnp.broadcast_to(streamed, (CB, CB)))
-        pair_scale[t] = column * (held[t] * time_scale)
-    sets = (far[:, W:W + CB].astype(F32), bins_ref[0].astype(F32),
-            jnp.where(first, bins_ref[1].astype(F32), far[:, W + CB:].astype(F32)), upper[:, W:].astype(F32))
-    for t, b in enumerate(sets):
-        if t % 2 == 0:
-            b = jnp.transpose(b)
-        h = jnp.floor(b * 0.5)
-        hi[t] = h
-        lo[t] = b - 2.0 * h
-    acc0[...] = jnp.zeros_like(acc0)
-    acc1[...] = jnp.zeros_like(acc1)
     iota = lax.broadcasted_iota(jnp.int32, (CB, CB), 0).astype(F32).astype(BF)
     one, zero = jnp.ones((CB, CB), BF), jnp.zeros((CB, CB), BF)
     sub = lax.broadcasted_iota(jnp.int32, (32, CB), 0) & 7
     slots = (0, flags[1], flags[2])
-    for k, block in enumerate((stream[...], lower[...], upper[:, :W])):
-        c0_ref[k] = lax.dot_general(pltpu.roll(block, 32, 1), shifted[slots[k], :CB, :], NT, preferred_element_type=F32)
-
-    def zscore(k, i):
-        rows = c_ref[k, 8 * i:8 * i + 8, :]
+
+    def zscore(k, i, local):
+        rows = c_first[pl.ds(pl.multiple_of(i * 8, 8), 8), :] if k == 0 else c_ref[k - 1, 8 * local:8 * local + 8, :]
         z = jnp.concatenate([rows[:, CB * p:CB * p + CB] for p in range(8)], 0)
-        return (z * pair_scale[k, i:i + 1, :]).astype(BF)
+        return (z * pair_scale[k, pl.ds(i, 1), :]).astype(BF)
 
     def low(t, i):
-        return jnp.broadcast_to(lo[t, i:i + 1, :], (64, CB)).astype(BF)
+        return jnp.broadcast_to(lo[t, pl.ds(i, 1), :], (64, CB)).astype(BF)
 
     def onehot(t, i):
-        return jnp.where(jnp.broadcast_to(hi[t, i:i + 1, :], (CB, CB)).astype(BF) == iota, one, zero)
-
-    def bin_group(base):
+        return jnp.where(jnp.broadcast_to(hi[t, pl.ds(i, 1), :], (CB, CB)).astype(BF) == iota, one, zero)
+
+    def bin_group(start, g):
+        base = pl.multiple_of(start + g * GROUP, GROUP)
         rows = pl.ds(base, GROUP)
         x = [c0_ref[k, rows, :] * pair_scale[k, rows, :] for k in range(3)]
         low8 = [lo[t, rows, :] for t in range(4)]
@@ -86,7 +68,7 @@
             i = base + ii
             e0 = jnp.where(sub == ii, extra0, 0.0).astype(BF)
             e1 = jnp.where(sub == ii, extra1, 0.0).astype(BF)
-            z = [zscore(k, i) for k in range(3)]
+            z = [zscore(k, i, g * GROUP + ii) for k in range(3)]
             left0.append(jnp.concatenate([z[0], z[0] * low(0, i), z[0] * low(1, i), e0], 0))
             left1.append(jnp.concatenate([z[1], z[1] * low(2, i), z[2], z[2] * low(3, i), e1], 0))
             right0.append(jnp.concatenate([onehot(0, i), onehot(1, i)], 0))
@@ -95,36 +77,70 @@
         acc0[...] += lax.dot_general(cat(left0), cat(right0), NT, preferred_element_type=F32)
         acc1[...] += lax.dot_general(cat(left1), cat(right1), NT, preferred_element_type=F32)
 
-    def bin_chunk(m):
-        for g in range(CHUNK // 8 // GROUP):
-            bin_group(m * (CHUNK // 8) + g * GROUP)
-
-    for m in range(1024 // CHUNK):
-        rows = slice(m * CHUNK, (m + 1) * CHUNK)
-        for k in range(3):
-            lags[k, rows, :] = lag_rows(wide.at[k], m * CHUNK // 8, CHUNK // 8)
-            c_ref[k, rows, :] = lax.dot_general(lags[k, rows, :], shifted[slots[k]], NT, preferred_element_type=F32)
-        if m > 0:
-            bin_chunk(m - 1)
-    bin_chunk(1024 // CHUNK - 1)
+    def prepare():
+        first, last = flags[1] == 1, flags[2] == 1
+        own, far_scale = scale_ref[0:1, :], scale_ref[1:2, :]
+        held = (far_scale, jnp.where(first, own, far_scale), jnp.where(last, own, far_scale))
+        for t, streamed in enumerate((own, scale_ref[2:3, :], scale_ref[3:4, :])):
+            column = jnp.transpose(jnp.broadcast_to(streamed, (CB, CB)))
+            pair_scale[t] = column * (held[t] * time_scale)
+        sets = (far[:, W:W + CB].astype(F32), bins_ref[0].astype(F32),
+                jnp.where(first, bins_ref[1].astype(F32), far[:, W + CB:].astype(F32)), upper[:, W:].astype(F32))
+        for t, b in enumerate(sets):
+            if t % 2 == 0:
+                b = jnp.transpose(b)
+            owner = jnp.floor(b * (1.0 / 16.0))
+            rest = b - 16.0 * owner
+            high_half = jnp.where(rest >= 8.0, 1.0, 0.0)
+            hi[t] = 8.0 * owner + rest - 8.0 * high_half
+            lo[t] = high_half
+        acc0[...] = jnp.zeros_like(acc0)
+        acc1[...] = jnp.zeros_like(acc1)
+        ahead = jnp.concatenate([pltpu.roll(far[:, :W], W - 32, 1), pltpu.roll(special[...], W - 32, 1)], 0)
+        for k, block in enumerate((stream[...], lower[...], upper[:, :W])):
+            pair = lax.dot_general(block, ahead, NT, preferred_element_type=F32)
+            c0_ref[k] = pair[:, :CB] if k == 0 else jnp.where(flags[k] == 1, pair[:, CB:], pair[:, :CB])
+
+    lag_a, lag_b, lag_c = (lags.at[k] for k in range(3))
+    half = 8 * STEP
+    lag_a[...] = lag_rows(wide.at[0], 0, STEP)
+    c_first[:half, :] = lax.dot_general(lag_a[...], shifted[0], NT, preferred_element_type=F32)
+    shift_rows(special[...], shifted.at[1])
+    lag_c[...] = lag_rows(wide.at[0], STEP, STEP)
+    c_first[half:, :] = lax.dot_general(lag_c[...], shifted[0], NT, preferred_element_type=F32)
+    prepare()
+    lag_b[...] = lag_rows(wide.at[1], 0, STEP)
+
+    def chunk(m, carry):
+        start = m * STEP
+        c_ref[0] = lax.dot_general(lag_b[...], shifted[slots[1]], NT, preferred_element_type=F32)
+        lag_c[...] = lag_rows(wide.at[2], start, STEP)
+        c_ref[1] = lax.dot_general(lag_c[...], shifted[slots[2]], NT, preferred_element_type=F32)
+        lag_b[...] = lag_rows(wide.at[1], lax.rem(start + STEP, CB), STEP)
+        for g in range(STEP // GROUP):
+            bin_group(start, g)
+        return carry
+
+    lax.fori_loop(0, CB // STEP, chunk, 0)
 
     total = lambda v: jnp.sum(v, axis=0, keepdims=True)
     forward = [acc0[0:64, :CB] + acc1[0:64, :CB], acc0[64:128, :CB] + acc1[64:128, :CB]]
     reverse = [acc0[0:64, CB:] + acc1[128:192, CB:], acc0[128:192, CB:] + acc1[192:256, CB:]]
     forward0 = [total(acc0[192:200, :CB]) + total(acc1[256:264, :CB]), total(acc0[200:208, :CB]) + total(acc1[264:272, :CB])]
     reverse0 = [total(acc0[192:200, CB:]) + total(acc1[272:280, CB:]), total(acc0[208:216, CB:]) + total(acc1[280:288, CB:])]
-    lag = lax.broadcasted_iota(jnp.int32, (CB, 64), 0)
-    r = lax.broadcasted_iota(jnp.int32, (CB, 64), 1)
+    lag = lax.broadcasted_iota(jnp.int32, (CB, CB), 0)
+    c = lax.broadcasted_iota(jnp.int32, (CB, CB), 1)
+    r = c & 63
     m = (r >> 3) * 8 + 8 - (r & 7)
-    to_forward = jnp.where(lag == m, 1.0, 0.0)
-    to_reverse = jnp.where(lag == 64 - m, 1.0, 0.0)
-    lag_row = lax.broadcasted_iota(jnp.int32, (CB, CB), 0)
-    parts = []
-    for q in range(2):
-        exact = lambda s, v: lax.dot_general(s, v, NN, precision=lax.Precision.HIGHEST, preferred_element_type=F32)
-        part = exact(to_forward, forward[q]) + exact(to_reverse, reverse[q])
-        part = part + jnp.where(lag_row == 0, forward0[q], 0.0) + jnp.where(lag_row == 64, reverse0[q], 0.0)
-        parts.append(part)
+    place = jnp.where(lag == jnp.where(c < 64, m, 64 - m), 1.0, 0.0).astype(BF)
+    rest = jnp.concatenate([jnp.concatenate([forward[q], reverse[q]], 0) for q in range(2)], 1)
+    both = jnp.zeros((CB, 2 * CB), F32)
+    for _piece in range(3):
+        piece = rest.astype(BF)
+        rest = rest - piece.astype(F32)
+        both = both + lax.dot_general(place, piece, NN, preferred_element_type=F32)
+    parts = [both[:, q * CB:q * CB + CB] + jnp.where(lag == 0, forward0[q], 0.0) + jnp.where(lag == 64, reverse0[q], 0.0)
+             for q in range(2)]
     out_ref[:, :CB] = jnp.transpose(parts[0] - parts[1])
     out_ref[:, CB:] = jnp.transpose(parts[1])
 
@@ -135,8 +151,8 @@
         in_specs=[SMEM] + [VMEM] * 7,
         out_specs=VMEM,
         out_shape=jax.ShapeDtypeStruct((CB, 2 * CB), F32),
-        scratch_shapes=[pltpu.VMEM((3, CB, W), F32), pltpu.VMEM((3, 1024, W), BF),
-                        pltpu.VMEM((2, 1024, W), BF), pltpu.VMEM((3, 1024, 1024), F32), pltpu.VMEM((3, CB, CB), F32),
+        scratch_shapes=[pltpu.VMEM((3, CB, W), F32), pltpu.VMEM((3, 8 * STEP, W), BF),
+                        pltpu.VMEM((2, 1024, W), BF), pltpu.VMEM((1024, 1024), F32), pltpu.VMEM((2, 8 * STEP, 1024), F32), pltpu.VMEM((3, CB, CB), F32),
                         pltpu.VMEM((3, CB, CB), F32), pltpu.VMEM((4, CB, CB), F32), pltpu.VMEM((4, CB, CB), F32),
                         pltpu.VMEM((224, 2 * CB), F32), pltpu.VMEM((288, 2 * CB), F32)],
         compiler_params=pltpu.CompilerParams(vmem_limit_bytes=36 << 20),
@@ -251,6 +267,24 @@
     )(gathered)
 
 
+def finish_kernel(scale, gathered, out_ref):
+    total = jnp.sum(gathered[...], axis=0) * scale
+    rows = jnp.concatenate([total[:, :CB], total[:, CB:]], 0)
+    out_ref[...] = jnp.transpose(rows)[:2 * MAX_LAG + 1, :]
+
+
+def finish(gathered, scale):
+    return pl.pallas_call(
+        functools.partial(finish_kernel, scale),
+        in_specs=[VMEM],
+        out_specs=VMEM,
+        out_shape=jax.ShapeDtypeStruct((2 * MAX_LAG + 1, 2 * gathered.shape[1]), F32),
+        compiler_params=pltpu.CompilerParams(vmem_limit_bytes=2 << 20),
+        cost_estimate=pl.CostEstimate(flops=1 << 15, bytes_accessed=1 << 17, transcendentals=0),
+        name="finish",
+    )(gathered)
+
+
 def exchange(block, source):
     n = lax.axis_size("chan")
     return lax.ppermute(block, "chan", [(source(i), i) for i in range(n)])
@@ -285,10 +319,9 @@
         slots = partial_stack.reshape(chan_count, CB // chan_count, 2 * CB)
         owned = jnp.sum(lax.all_to_all(slots, "chan", 0, 0, tiled=True), axis=0)
         copies = jnp.broadcast_to(owned[None], (seg_count,) + owned.shape)
-        owned = jnp.sum(lax.all_to_all(copies, "seg", 0, 0, tiled=True), axis=0)
-    pair_total = ROUNDS * chan_count * CB * CB // NB
-    owned = owned.reshape(-1, 2, CB)[:, :, :2 * MAX_LAG + 1] * (1.0 / math.sqrt(pair_total))
-    return jnp.transpose(owned, (2, 0, 1)).reshape(2 * MAX_LAG + 1, -1)
+        gathered = lax.all_to_all(copies, "seg", 0, 0, tiled=True)
+        pair_total = ROUNDS * chan_count * CB * CB // NB
+        return finish(gathered, 1.0 / math.sqrt(pair_total))
 
 
 def solution(mesh):

time: 74.4 us -> 72.2 us (0.970)
  Pallas kernels: 19 us -> 16.7 us
    pallas_call x1, Pallas kernels: 17.9 us -> 15.5 us  [fused(): pl.pallas_call(functools.partial(fused_kernel, time_scale), in_specs=[SME...]
where the time goes in v3:
time: 72.2 us; the launch traced here: 72 us
  blocking collectives  42.8 us (59%)
  Pallas kernels  16.7 us (23%)
  starting transfers between devices  9.62 us (13%)
  local copies, waits for them, and re-layouts  2.64 us (4%)
    all_to_all x1, blocking collectives, local(): lax.all_to_all(copies_of(rows, seg_count), 'seg', 0, 0, tiled=True)  16.7 us
    pallas_call x1, Pallas kernels, fused(): pl.pallas_call(functools.partial(fused_kernel, time_scale), in_specs=[SME...  15.5 us
    all_to_all x1, blocking collectives, local(): owned = jnp.sum(lax.all_to_all(slots, 'chan', 0, 0, tiled=True), axis=0)  13.6 us
    all_to_all x1, blocking collectives, local(): gathered = lax.all_to_all(copies, 'seg', 0, 0, tiled=True)  12.5 us
    ppermute x6, starting transfers between devices, exchange(): return lax.ppermute(block, 'chan', [(source(i), i) for i in range(n)])  9.62 us
    unnamed x8, local copies, waits for them, and re-layouts  1.96 us
  transfers between devices with their start and end apart: 6, of which 0 were waited for; matrix products, arithmetic and copies ran while one was open for 0% of the time, Pallas kernels for 1%

profile of v3, /device:TPU:1, one launch (start us, length us, event | category | flops | bytes accessed | tf_op | source)
XLA Modules:
  0.0 72.0 jit_solution(14468645244210214998)
XLA Ops:
  0.0 0.0 copy-start
  0.0 1.0 %copy-done = bf16[128,2048]{1,0:T(8,128)(2,1)S(1)} copy-done((bf16[128,2048]{1,0:T(8,128)(2,1)S(1)}, bf16[128,2048]{1,0:T(8,128)(2,1)}, u32[]{:S(2)}) %copy-start) | copy-done | bytes 524312
  1.0 0.0 copy-start.1
  1.0 0.2 square_sums.1.squares.refs_0_
  1.2 2.2 %collective-permute-start = (f32[1,128]{1,0:T(1,128)S(1)}, f32[1,128]{1,0:T(1,128)S(1)}, u32[]{:S(2)}, u32[]{:S(2)}) collective-permute-start(f32[1,128]{1,0:T(1,128)S(1)} %square_sums.1.squares.refs_0_), channel_id=1, source_target_pairs={{128,0},{144,16},{160,32},{176,48},{192,64},{208,80},{224,96},{240... | collective-permute-start | bytes 1544 | tf_op jit(solution)/shard_map/send_squares/ppermute | solution.py:290
  3.4 1.6 %collective-permute-start.1 = (f32[1,128]{1,0:T(1,128)S(1)}, f32[1,128]{1,0:T(1,128)S(1)}, u32[]{:S(2)}, u32[]{:S(2)}) collective-permute-start(f32[1,128]{1,0:T(1,128)S(1)} %square_sums.1.squares.refs_0_), channel_id=1, source_target_pairs={{112,0},{0,16},{16,32},{32,48},{48,64},{64,80},{80,96},{96,112},{2... | collective-permute-start | bytes 1544 | tf_op jit(solution)/shard_map/send_squares/ppermute | solution.py:290
  5.1 3.9 %collective-permute-start.2 = (f32[1,128]{1,0:T(1,128)S(1)}, f32[1,128]{1,0:T(1,128)S(1)}, u32[]{:S(2)}, u32[]{:S(2)}) collective-permute-start(f32[1,128]{1,0:T(1,128)S(1)} %square_sums.1.squares.refs_0_), channel_id=1, source_target_pairs={{16,0},{32,16},{48,32},{64,48},{80,64},{96,80},{112,96},{0,112},{1... | collective-permute-start | bytes 1544 | tf_op jit(solution)/shard_map/send_squares/ppermute | solution.py:290
  9.0 0.1 pad_add_fusion.flags
  9.1 0.0 copy-done.1
  9.1 0.0 copy-start.2
  9.1 0.9 %copy-done.2 = s32[2,128,128]{2,1,0:T(8,128)S(1)} copy-done((s32[2,128,128]{2,1,0:T(8,128)S(1)}, s32[2,128,128]{2,1,0:T(8,128)}, u32[]{:S(2)}) %copy-start.2) | copy-done | bytes 131096
  10.0 0.9 %payloads.1 = (bf16[128,1152]{1,0:T(8,128)(2,1)S(1)}, bf16[128,1408]{1,0:T(8,128)(2,1)S(1)}, bf16[128,1280]{1,0:T(8,128)(2,1)S(1)}, bf16[128,1152]{1,0:T(8,128)(2,1)S(1)}) custom-call(s32[3]{0:T(128)S(1)} %pad_add_fusion.flags, f32[1,128]{1,0:T(1,128)S(1)} %square_sums.1.squares.refs_0_, bf16[128,2048]{1,0:T(8,128)(2,1)S(1)} %copy-done.1, ...), custom_call_target="tpu_custom_call" | custom-call | flops 262144 | bytes 2097152 | tf_op jit(solution)/shard_map/payloads/pallas_call | solution.py:205
  10.9 0.0 copy-start.3
  10.9 0.0 collective-permute-done.refs_1_
  10.9 0.0 collective-permute-done.1.refs_2_
  10.9 0.0 collective-permute-done.2.refs_3_
  11.0 0.3 collective-permute-start.5
  11.2 1.6 %collective-permute-start.4 = (bf16[128,1280]{1,0:T(8,128)(2,1)S(1)}, bf16[128,1280]{1,0:T(8,128)(2,1)S(1)}, u32[]{:S(2)}, u32[]{:S(2)}) collective-permute-start(bf16[128,1280]{1,0:T(8,128)(2,1)S(1)} %get-tuple-element.24), channel_id=1, source_target_pairs={{16,0},{32,16},{48,32},{64,48},{80,64},{96,80},{112,96},{0,112},{1... | collective-permute-start | bytes 983048 | tf_op jit(solution)/shard_map/send_blocks/ppermute | solution.py:290
  12.8 0.0 collective-permute-start.3
  12.8 16.7 %all_to_all.15.gathered = f32[16,4,128]{2,1,0:T(4,128)S(1)} all-to-all(f32[16,4,128]{2,1,0:T(4,128)S(1)} %square_copies.1), channel_id=1, replica_groups=mesh['chan'=16,'seg'=16] {'seg'}, dimensions={0} | all-to-all | bytes 65536 | tf_op jit(solution)/shard_map/energies/all_to_all | solution.py:314
  29.5 0.0 collective-permute-done.3.lower
  29.5 0.0 collective-permute-done.4.upper
  29.5 0.0 collective-permute-done.5.far
  29.6 0.0 copy-done.3
  29.6 15.5 %lags_and_bins.1 = f32[128,256]{1,0:T(8,128)S(1)} custom-call(s32[3]{0:T(128)S(1)} %pad_add_fusion.flags, f32[4,128]{1,0:T(4,128)S(1)} %inverse_rms.1.scale_ref, s32[2,128,128]{2,1,0:T(8,128)S(1)} %copy-done.3, bf16[128,1152]{1,0:T(8,128)(2,1)S(1)} %get-tuple-element.23.stream, bf16[128,1152]{1,0:T(8,128)(2,1)S(1)} %collective-permute-done.3.lower, ...), custom_call_target="tpu_custom_call" | custom-call | flops 9663676416 | bytes 6291456 | tf_op jit(solution)/shard_map/lags_and_bins/pallas_call | solution.py:149
  45.1 13.6 %all_to_all.16 = f32[16,8,256]{2,1,0:T(8,128)S(1)} all-to-all(f32[16,8,256]{2,1,0:T(8,128)S(1)} %bitcast.4), channel_id=1, replica_groups=mesh['chan'=16,'seg'=16] {'chan'}, dimensions={0} | all-to-all | bytes 262144 | tf_op jit(solution)/shard_map/reduce_bins/all_to_all | solution.py:320
  58.7 12.5 %all_to_all.17.gathered = f32[16,8,256]{2,1,0:T(8,128)S(1)} all-to-all(f32[16,8,256]{2,1,0:T(8,128)S(1)} %broadcast_in_dim.2), channel_id=1, replica_groups=mesh['chan'=16,'seg'=16] {'seg'}, dimensions={0} | all-to-all | bytes 262144 | tf_op jit(solution)/shard_map/reduce_bins/all_to_all | solution.py:322
  71.2 0.1 finish.1
  71.3 0.7 copy.3
  (4 shorter events, 0.1 us)
Async XLA Ops:
  0.0 1.0 %copy-start = (bf16[128,2048]{1,0:T(8,128)(2,1)S(1)}, bf16[128,2048]{1,0:T(8,128)(2,1)}, u32[]{:S(2)}) copy-start(bf16[128,2048]{1,0:T(8,128)(2,1)} %traces.3) | copy-start | bytes 1572868
  1.0 8.0 %copy-start.1 = (bf16[128,2048]{1,0:T(8,128)(2,1)S(1)}, bf16[128,2048]{1,0:T(8,128)(2,1)}, u32[]{:S(2)}) copy-start(bf16[128,2048]{1,0:T(8,128)(2,1)} %traces.3) | copy-start | bytes 1572868
  1.2 9.7 %collective-permute-start = (f32[1,128]{1,0:T(1,128)S(1)}, f32[1,128]{1,0:T(1,128)S(1)}, u32[]{:S(2)}, u32[]{:S(2)}) collective-permute-start(f32[1,128]{1,0:T(1,128)S(1)} %square_sums.1.squares.refs_0_), channel_id=1, source_target_pairs={{128,0},{144,16},{160,32},{176,48},{192,64},{208,80},{224,96},{240... | collective-permute-start | bytes 1544 | tf_op jit(solution)/shard_map/send_squares/ppermute | solution.py:290
  3.4 7.5 %collective-permute-start.1 = (f32[1,128]{1,0:T(1,128)S(1)}, f32[1,128]{1,0:T(1,128)S(1)}, u32[]{:S(2)}, u32[]{:S(2)}) collective-permute-start(f32[1,128]{1,0:T(1,128)S(1)} %square_sums.1.squares.refs_0_), channel_id=1, source_target_pairs={{112,0},{0,16},{16,32},{32,48},{48,64},{64,80},{80,96},{96,112},{2... | collective-permute-start | bytes 1544 | tf_op jit(solution)/shard_map/send_squares/ppermute | solution.py:290
  5.1 5.9 %collective-permute-start.2 = (f32[1,128]{1,0:T(1,128)S(1)}, f32[1,128]{1,0:T(1,128)S(1)}, u32[]{:S(2)}, u32[]{:S(2)}) collective-permute-start(f32[1,128]{1,0:T(1,128)S(1)} %square_sums.1.squares.refs_0_), channel_id=1, source_target_pairs={{16,0},{32,16},{48,32},{64,48},{80,64},{96,80},{112,96},{0,112},{1... | collective-permute-start | bytes 1544 | tf_op jit(solution)/shard_map/send_squares/ppermute | solution.py:290
  9.1 0.9 %copy-start.2 = (s32[2,128,128]{2,1,0:T(8,128)S(1)}, s32[2,128,128]{2,1,0:T(8,128)}, u32[]{:S(2)}) copy-start(s32[2,128,128]{2,1,0:T(8,128)} %bins_ref.1) | copy-start | bytes 393220
  10.9 18.6 %copy-start.3 = (s32[2,128,128]{2,1,0:T(8,128)S(1)}, s32[2,128,128]{2,1,0:T(8,128)}, u32[]{:S(2)}) copy-start(s32[2,128,128]{2,1,0:T(8,128)} %bins_ref.1) | copy-start | bytes 393220
  11.0 18.6 %collective-permute-start.5 = (bf16[128,1408]{1,0:T(8,128)(2,1)S(1)}, bf16[128,1408]{1,0:T(8,128)(2,1)S(1)}, u32[]{:S(2)}, u32[]{:S(2)}) collective-permute-start(bf16[128,1408]{1,0:T(8,128)(2,1)S(1)} %get-tuple-element.25), channel_id=1, source_target_pairs={{128,0},{144,16},{160,32},{176,48},{192,64},{208,80},{224,96},{240... | collective-permute-start | bytes 1081352 | tf_op jit(solution)/shard_map/send_blocks/ppermute | solution.py:290
  11.2 18.3 %collective-permute-start.4 = (bf16[128,1280]{1,0:T(8,128)(2,1)S(1)}, bf16[128,1280]{1,0:T(8,128)(2,1)S(1)}, u32[]{:S(2)}, u32[]{:S(2)}) collective-permute-start(bf16[128,1280]{1,0:T(8,128)(2,1)S(1)} %get-tuple-element.24), channel_id=1, source_target_pairs={{16,0},{32,16},{48,32},{64,48},{80,64},{96,80},{112,96},{0,112},{1... | collective-permute-start | bytes 983048 | tf_op jit(solution)/shard_map/send_blocks/ppermute | solution.py:290
  12.8 16.7 %collective-permute-start.3 = (bf16[128,1152]{1,0:T(8,128)(2,1)S(1)}, bf16[128,1152]{1,0:T(8,128)(2,1)S(1)}, u32[]{:S(2)}, u32[]{:S(2)}) collective-permute-start(bf16[128,1152]{1,0:T(8,128)(2,1)S(1)} %get-tuple-element.23.stream), channel_id=1, source_target_pairs={{112,0},{0,16},{16,32},{32,48},{48,64},{64,80},{80,96},{96,112},{2... | collective-permute-start | bytes 884744 | tf_op jit(solution)/shard_map/send_blocks/ppermute | solution.py:290

commit v4 on v3

--- a/solution.py
+++ b/solution.py
@@ -270,7 +270,7 @@
 def finish_kernel(scale, gathered, out_ref):
     total = jnp.sum(gathered[...], axis=0) * scale
     rows = jnp.concatenate([total[:, :CB], total[:, CB:]], 0)
-    out_ref[...] = jnp.transpose(rows)[:2 * MAX_LAG + 1, :]
+    out_ref[...] = rows[:, :2 * MAX_LAG + 1]
 
 
 def finish(gathered, scale):
@@ -278,7 +278,7 @@
         functools.partial(finish_kernel, scale),
         in_specs=[VMEM],
         out_specs=VMEM,
-        out_shape=jax.ShapeDtypeStruct((2 * MAX_LAG + 1, 2 * gathered.shape[1]), F32),
+        out_shape=jax.ShapeDtypeStruct((2 * gathered.shape[1], 2 * MAX_LAG + 1), F32),
         compiler_params=pltpu.CompilerParams(vmem_limit_bytes=2 << 20),
         cost_estimate=pl.CostEstimate(flops=1 << 15, bytes_accessed=1 << 17, transcendentals=0),
         name="finish",
@@ -321,7 +321,7 @@
         copies = jnp.broadcast_to(owned[None], (seg_count,) + owned.shape)
         gathered = lax.all_to_all(copies, "seg", 0, 0, tiled=True)
         pair_total = ROUNDS * chan_count * CB * CB // NB
-        return finish(gathered, 1.0 / math.sqrt(pair_total))
+        return jnp.transpose(finish(gathered, 1.0 / math.sqrt(pair_total)))
 
 
 def solution(mesh):

time: 72.2 us -> 72.1 us (level)
  no operation moved by 1% of the time
where the time goes in v4:
time: 72.1 us; the launch traced here: 71.8 us
  blocking collectives  42.8 us (59%)
  Pallas kernels  17.2 us (24%)
  starting transfers between devices  9.62 us (13%)
  local copies, waits for them, and re-layouts  1.97 us (3%)
    all_to_all x1, blocking collectives, local(): lax.all_to_all(copies_of(rows, seg_count), 'seg', 0, 0, tiled=True)  16.7 us
    pallas_call x1, Pallas kernels, fused(): pl.pallas_call(functools.partial(fused_kernel, time_scale), in_specs=[SME...  15.5 us
    all_to_all x1, blocking collectives, local(): owned = jnp.sum(lax.all_to_all(slots, 'chan', 0, 0, tiled=True), axis=0)  13.6 us
    all_to_all x1, blocking collectives, local(): gathered = lax.all_to_all(copies, 'seg', 0, 0, tiled=True)  12.5 us
    ppermute x6, starting transfers between devices, exchange(): return lax.ppermute(block, 'chan', [(source(i), i) for i in range(n)])  9.62 us
    unnamed x8, local copies, waits for them, and re-layouts  1.96 us
  transfers between devices with their start and end apart: 6, of which 0 were waited for; matrix products, arithmetic and copies ran while one was open for 0% of the time, Pallas kernels for 1%

profile of v4, /device:TPU:1, one launch (start us, length us, event | category | flops | bytes accessed | tf_op | source)
XLA Modules:
  0.0 71.8 jit_solution(12826760529278377957)
XLA Ops:
  0.0 0.0 copy-start
  0.0 1.0 %copy-done = bf16[128,2048]{1,0:T(8,128)(2,1)S(1)} copy-done((bf16[128,2048]{1,0:T(8,128)(2,1)S(1)}, bf16[128,2048]{1,0:T(8,128)(2,1)}, u32[]{:S(2)}) %copy-start) | copy-done | bytes 524312
  1.0 0.0 copy-start.1
  1.0 0.2 square_sums.1.squares.refs_0_
  1.2 2.2 %collective-permute-start = (f32[1,128]{1,0:T(1,128)S(1)}, f32[1,128]{1,0:T(1,128)S(1)}, u32[]{:S(2)}, u32[]{:S(2)}) collective-permute-start(f32[1,128]{1,0:T(1,128)S(1)} %square_sums.1.squares.refs_0_), channel_id=1, source_target_pairs={{128,0},{144,16},{160,32},{176,48},{192,64},{208,80},{224,96},{240... | collective-permute-start | bytes 1544 | tf_op jit(solution)/shard_map/send_squares/ppermute | solution.py:290
  3.4 1.6 %collective-permute-start.1 = (f32[1,128]{1,0:T(1,128)S(1)}, f32[1,128]{1,0:T(1,128)S(1)}, u32[]{:S(2)}, u32[]{:S(2)}) collective-permute-start(f32[1,128]{1,0:T(1,128)S(1)} %square_sums.1.squares.refs_0_), channel_id=1, source_target_pairs={{112,0},{0,16},{16,32},{32,48},{48,64},{64,80},{80,96},{96,112},{2... | collective-permute-start | bytes 1544 | tf_op jit(solution)/shard_map/send_squares/ppermute | solution.py:290
  5.1 3.9 %collective-permute-start.2 = (f32[1,128]{1,0:T(1,128)S(1)}, f32[1,128]{1,0:T(1,128)S(1)}, u32[]{:S(2)}, u32[]{:S(2)}) collective-permute-start(f32[1,128]{1,0:T(1,128)S(1)} %square_sums.1.squares.refs_0_), channel_id=1, source_target_pairs={{16,0},{32,16},{48,32},{64,48},{80,64},{96,80},{112,96},{0,112},{1... | collective-permute-start | bytes 1544 | tf_op jit(solution)/shard_map/send_squares/ppermute | solution.py:290
  9.0 0.1 pad_add_fusion.flags
  9.1 0.0 copy-done.1
  9.1 0.0 copy-start.2
  9.1 0.9 %copy-done.2 = s32[2,128,128]{2,1,0:T(8,128)S(1)} copy-done((s32[2,128,128]{2,1,0:T(8,128)S(1)}, s32[2,128,128]{2,1,0:T(8,128)}, u32[]{:S(2)}) %copy-start.2) | copy-done | bytes 131096
  10.0 0.9 %payloads.1 = (bf16[128,1152]{1,0:T(8,128)(2,1)S(1)}, bf16[128,1408]{1,0:T(8,128)(2,1)S(1)}, bf16[128,1280]{1,0:T(8,128)(2,1)S(1)}, bf16[128,1152]{1,0:T(8,128)(2,1)S(1)}) custom-call(s32[3]{0:T(128)S(1)} %pad_add_fusion.flags, f32[1,128]{1,0:T(1,128)S(1)} %square_sums.1.squares.refs_0_, bf16[128,2048]{1,0:T(8,128)(2,1)S(1)} %copy-done.1, ...), custom_call_target="tpu_custom_call" | custom-call | flops 262144 | bytes 2097152 | tf_op jit(solution)/shard_map/payloads/pallas_call | solution.py:205
  10.9 0.0 copy-start.3
  10.9 0.0 collective-permute-done.refs_1_
  10.9 0.0 collective-permute-done.1.refs_2_
  10.9 0.0 collective-permute-done.2.refs_3_
  11.0 0.3 collective-permute-start.5
  11.2 1.6 %collective-permute-start.4 = (bf16[128,1280]{1,0:T(8,128)(2,1)S(1)}, bf16[128,1280]{1,0:T(8,128)(2,1)S(1)}, u32[]{:S(2)}, u32[]{:S(2)}) collective-permute-start(bf16[128,1280]{1,0:T(8,128)(2,1)S(1)} %get-tuple-element.24), channel_id=1, source_target_pairs={{16,0},{32,16},{48,32},{64,48},{80,64},{96,80},{112,96},{0,112},{1... | collective-permute-start | bytes 983048 | tf_op jit(solution)/shard_map/send_blocks/ppermute | solution.py:290
  12.8 0.0 collective-permute-start.3
  12.8 16.7 %all_to_all.15.gathered = f32[16,4,128]{2,1,0:T(4,128)S(1)} all-to-all(f32[16,4,128]{2,1,0:T(4,128)S(1)} %square_copies.1), channel_id=1, replica_groups=mesh['chan'=16,'seg'=16] {'seg'}, dimensions={0} | all-to-all | bytes 65536 | tf_op jit(solution)/shard_map/energies/all_to_all | solution.py:314
  29.5 0.0 collective-permute-done.3.lower
  29.5 0.0 collective-permute-done.4.upper
  29.5 0.0 collective-permute-done.5.far
  29.6 0.0 copy-done.3
  29.6 15.5 %lags_and_bins.1 = f32[128,256]{1,0:T(8,128)S(1)} custom-call(s32[3]{0:T(128)S(1)} %pad_add_fusion.flags, f32[4,128]{1,0:T(4,128)S(1)} %inverse_rms.1.scale_ref, s32[2,128,128]{2,1,0:T(8,128)S(1)} %copy-done.3, bf16[128,1152]{1,0:T(8,128)(2,1)S(1)} %get-tuple-element.23.stream, bf16[128,1152]{1,0:T(8,128)(2,1)S(1)} %collective-permute-done.3.lower, ...), custom_call_target="tpu_custom_call" | custom-call | flops 9663676416 | bytes 6291456 | tf_op jit(solution)/shard_map/lags_and_bins/pallas_call | solution.py:149
  45.1 13.6 %all_to_all.16 = f32[16,8,256]{2,1,0:T(8,128)S(1)} all-to-all(f32[16,8,256]{2,1,0:T(8,128)S(1)} %bitcast.5), channel_id=1, replica_groups=mesh['chan'=16,'seg'=16] {'chan'}, dimensions={0} | all-to-all | bytes 262144 | tf_op jit(solution)/shard_map/reduce_bins/all_to_all | solution.py:320
  58.7 12.5 %all_to_all.17.gathered = f32[16,8,256]{2,1,0:T(8,128)S(1)} all-to-all(f32[16,8,256]{2,1,0:T(8,128)S(1)} %broadcast_in_dim.2), channel_id=1, replica_groups=mesh['chan'=16,'seg'=16] {'seg'}, dimensions={0} | all-to-all | bytes 262144 | tf_op jit(solution)/shard_map/reduce_bins/all_to_all | solution.py:322
  71.2 0.6 finish.1
  (4 shorter events, 0.1 us)
Async XLA Ops:
  0.0 1.0 %copy-start = (bf16[128,2048]{1,0:T(8,128)(2,1)S(1)}, bf16[128,2048]{1,0:T(8,128)(2,1)}, u32[]{:S(2)}) copy-start(bf16[128,2048]{1,0:T(8,128)(2,1)} %traces.3) | copy-start | bytes 1572868
  1.0 8.0 %copy-start.1 = (bf16[128,2048]{1,0:T(8,128)(2,1)S(1)}, bf16[128,2048]{1,0:T(8,128)(2,1)}, u32[]{:S(2)}) copy-start(bf16[128,2048]{1,0:T(8,128)(2,1)} %traces.3) | copy-start | bytes 1572868
  1.2 9.7 %collective-permute-start = (f32[1,128]{1,0:T(1,128)S(1)}, f32[1,128]{1,0:T(1,128)S(1)}, u32[]{:S(2)}, u32[]{:S(2)}) collective-permute-start(f32[1,128]{1,0:T(1,128)S(1)} %square_sums.1.squares.refs_0_), channel_id=1, source_target_pairs={{128,0},{144,16},{160,32},{176,48},{192,64},{208,80},{224,96},{240... | collective-permute-start | bytes 1544 | tf_op jit(solution)/shard_map/send_squares/ppermute | solution.py:290
  3.4 7.5 %collective-permute-start.1 = (f32[1,128]{1,0:T(1,128)S(1)}, f32[1,128]{1,0:T(1,128)S(1)}, u32[]{:S(2)}, u32[]{:S(2)}) collective-permute-start(f32[1,128]{1,0:T(1,128)S(1)} %square_sums.1.squares.refs_0_), channel_id=1, source_target_pairs={{112,0},{0,16},{16,32},{32,48},{48,64},{64,80},{80,96},{96,112},{2... | collective-permute-start | bytes 1544 | tf_op jit(solution)/shard_map/send_squares/ppermute | solution.py:290
  5.1 5.9 %collective-permute-start.2 = (f32[1,128]{1,0:T(1,128)S(1)}, f32[1,128]{1,0:T(1,128)S(1)}, u32[]{:S(2)}, u32[]{:S(2)}) collective-permute-start(f32[1,128]{1,0:T(1,128)S(1)} %square_sums.1.squares.refs_0_), channel_id=1, source_target_pairs={{16,0},{32,16},{48,32},{64,48},{80,64},{96,80},{112,96},{0,112},{1... | collective-permute-start | bytes 1544 | tf_op jit(solution)/shard_map/send_squares/ppermute | solution.py:290
  9.1 0.9 %copy-start.2 = (s32[2,128,128]{2,1,0:T(8,128)S(1)}, s32[2,128,128]{2,1,0:T(8,128)}, u32[]{:S(2)}) copy-start(s32[2,128,128]{2,1,0:T(8,128)} %bins_ref.1) | copy-start | bytes 393220
  10.9 18.6 %copy-start.3 = (s32[2,128,128]{2,1,0:T(8,128)S(1)}, s32[2,128,128]{2,1,0:T(8,128)}, u32[]{:S(2)}) copy-start(s32[2,128,128]{2,1,0:T(8,128)} %bins_ref.1) | copy-start | bytes 393220
  11.0 18.6 %collective-permute-start.5 = (bf16[128,1408]{1,0:T(8,128)(2,1)S(1)}, bf16[128,1408]{1,0:T(8,128)(2,1)S(1)}, u32[]{:S(2)}, u32[]{:S(2)}) collective-permute-start(bf16[128,1408]{1,0:T(8,128)(2,1)S(1)} %get-tuple-element.25), channel_id=1, source_target_pairs={{128,0},{144,16},{160,32},{176,48},{192,64},{208,80},{224,96},{240... | collective-permute-start | bytes 1081352 | tf_op jit(solution)/shard_map/send_blocks/ppermute | solution.py:290
  11.2 18.3 %collective-permute-start.4 = (bf16[128,1280]{1,0:T(8,128)(2,1)S(1)}, bf16[128,1280]{1,0:T(8,128)(2,1)S(1)}, u32[]{:S(2)}, u32[]{:S(2)}) collective-permute-start(bf16[128,1280]{1,0:T(8,128)(2,1)S(1)} %get-tuple-element.24), channel_id=1, source_target_pairs={{16,0},{32,16},{48,32},{64,48},{80,64},{96,80},{112,96},{0,112},{1... | collective-permute-start | bytes 983048 | tf_op jit(solution)/shard_map/send_blocks/ppermute | solution.py:290
  12.8 16.7 %collective-permute-start.3 = (bf16[128,1152]{1,0:T(8,128)(2,1)S(1)}, bf16[128,1152]{1,0:T(8,128)(2,1)S(1)}, u32[]{:S(2)}, u32[]{:S(2)}) collective-permute-start(bf16[128,1152]{1,0:T(8,128)(2,1)S(1)} %get-tuple-element.23.stream), channel_id=1, source_target_pairs={{112,0},{0,16},{16,32},{32,48},{48,64},{64,80},{80,96},{96,112},{2... | collective-permute-start | bytes 884744 | tf_op jit(solution)/shard_map/send_blocks/ppermute | solution.py:290

commit v5 on v4

--- a/solution.py
+++ b/solution.py
@@ -12,6 +12,7 @@
 NN = (((1,), (0,)), ((), ()))
 F32, BF = jnp.float32, jnp.bfloat16
 W = 1152
+EPSILON = 1e-06
 CB = 128
 VMEM = pl.BlockSpec(memory_space=pltpu.VMEM)
 SMEM = pl.BlockSpec(memory_space=pltpu.SMEM)
@@ -34,7 +35,7 @@
 STEP = 64
 
 
-def fused_kernel(time_scale, flags, scale_ref, bins_ref, stream, lower, upper, far, special, out_ref,
+def fused_kernel(total_time, flags, squares, bins_ref, stream, lower, upper, far, special, out_ref,
                  wide, lags, shifted, c_first, c_ref, c0_ref, pair_scale, hi, lo, acc0, acc1):
     shift_rows(far[:, :W], shifted.at[0])
     wide[0] = stream[...].astype(F32)
@@ -79,11 +80,16 @@
 
     def prepare():
         first, last = flags[1] == 1, flags[2] == 1
-        own, far_scale = scale_ref[0:1, :], scale_ref[1:2, :]
+        count = squares.shape[0] // 2
+        low, high = jnp.sum(squares[:count], axis=0), jnp.sum(squares[count:], axis=0)
+        home = jnp.where(flags[0] == 1, high, low)
+        inverse_rms = lambda v: lax.rsqrt(v / total_time + EPSILON)
+        near = inverse_rms(home)
+        own, far_scale = near[0:1], inverse_rms(jnp.where(flags[0] == 1, low, high)[0:1])
         held = (far_scale, jnp.where(first, own, far_scale), jnp.where(last, own, far_scale))
-        for t, streamed in enumerate((own, scale_ref[2:3, :], scale_ref[3:4, :])):
+        for t, streamed in enumerate((own, near[1:2], near[2:3])):
             column = jnp.transpose(jnp.broadcast_to(streamed, (CB, CB)))
-            pair_scale[t] = column * (held[t] * time_scale)
+            pair_scale[t] = column * (held[t] * (1.0 / math.sqrt(total_time)))
         sets = (far[:, W:W + CB].astype(F32), bins_ref[0].astype(F32),
                 jnp.where(first, bins_ref[1].astype(F32), far[:, W + CB:].astype(F32)), upper[:, W:].astype(F32))
         for t, b in enumerate(sets):
@@ -145,9 +151,9 @@
     out_ref[:, CB:] = jnp.transpose(parts[1])
 
 
-def fused(flags, scales, bins, stream, lower, upper, far, special, time_scale):
-    return pl.pallas_call(
-        functools.partial(fused_kernel, time_scale),
+def fused(flags, squares, bins, stream, lower, upper, far, special, total_time):
+    return pl.pallas_call(
+        functools.partial(fused_kernel, total_time),
         in_specs=[SMEM] + [VMEM] * 7,
         out_specs=VMEM,
         out_shape=jax.ShapeDtypeStruct((CB, 2 * CB), F32),
@@ -158,13 +164,12 @@
         compiler_params=pltpu.CompilerParams(vmem_limit_bytes=36 << 20),
         cost_estimate=pl.CostEstimate(flops=4 * 2 * 1024 * 1024 * W, bytes_accessed=6 << 20, transcendentals=0),
         name="lags_and_bins",
-    )(flags, scales, bins, stream, lower, upper, far, special)
+    )(flags, squares, bins, stream, lower, upper, far, special)
 
 
 MAX_LAG = 32
 NB = 256
 ROUNDS = 2
-EPSILON = 1e-06
 HALF = 1024
 
 
@@ -251,22 +256,6 @@
     )(*rows)
 
 
-def inverse_rms_kernel(total_time, gathered, out_ref):
-    out_ref[...] = lax.rsqrt(jnp.sum(gathered[...], axis=0) / total_time + EPSILON)
-
-
-def inverse_rms(gathered, total_time):
-    return pl.pallas_call(
-        functools.partial(inverse_rms_kernel, total_time),
-        in_specs=[VMEM],
-        out_specs=VMEM,
-        out_shape=jax.ShapeDtypeStruct((4, CB), F32),
-        compiler_params=pltpu.CompilerParams(vmem_limit_bytes=2 << 20),
-        cost_estimate=pl.CostEstimate(flops=1 << 12, bytes_accessed=1 << 13, transcendentals=0),
-        name="inverse_rms",
-    )(gathered)
-
-
 def finish_kernel(scale, gathered, out_ref):
     total = jnp.sum(gathered[...], axis=0) * scale
     rows = jnp.concatenate([total[:, :CB], total[:, CB:]], 0)
@@ -304,17 +293,17 @@
     squares = square_sums(traces)
     stream, far_payload, upper_payload, special = payloads(flags, squares, traces, pair_bins)
     with jax.named_scope("send_squares"):
-        rows = [squares] + [exchange(squares, source) for source in (FAR, LOWER, UPPER)]
+        rows = [squares] + [exchange(squares, source) for source in (LOWER, UPPER)]
     rows, stream, far_payload, upper_payload = lax.optimization_barrier((rows, stream, far_payload, upper_payload))
     with jax.named_scope("send_blocks"):
         far = exchange(far_payload, FAR)
         lower = exchange(stream, LOWER)
         upper = exchange(upper_payload, UPPER)
     with jax.named_scope("energies"):
-        gathered = lax.all_to_all(copies_of(rows, seg_count), "seg", 0, 0, tiled=True)
-        scales = inverse_rms(gathered, total_time)
-    partial_stack = fused(flags, scales, pair_bins, stream, lower, upper, far, special,
-                          1.0 / math.sqrt(total_time))
+        block = lambda c: [c * seg_count + n for n in range(seg_count)]
+        groups = [block(c) + block(FAR(c)) for c in range(chan_count // 2)]
+        gathered = lax.all_to_all(copies_of(rows, 2 * seg_count), ("chan", "seg"), 0, 0, tiled=True, axis_index_groups=groups)
+    partial_stack = fused(flags, gathered, pair_bins, stream, lower, upper, far, special, total_time)
     with jax.named_scope("reduce_bins"):
         slots = partial_stack.reshape(chan_count, CB // chan_count, 2 * CB)
         owned = jnp.sum(lax.all_to_all(slots, "chan", 0, 0, tiled=True), axis=0)

time: 72.1 us -> 72.2 us (level)
    all_to_all x1, blocking collectives: 12.5 us -> 13.3 us  [local(): gathered = lax.all_to_all(copies, 'seg', 0, 0, tiled=True)]
    ppermute x6 -> x5, starting transfers between devices: 9.62 us -> 9.53 us  [exchange(): return lax.ppermute(block, 'chan', [(source(i), i) for i in range(n)])]
    pallas_call x2 -> x1, Pallas kernels: 15.5 us -> 15.5 us  [fused(): pl.pallas_call(functools.partial(fused_kernel, total_time), in_specs=[SME...]
  transfers between devices with their start and end apart: 6 -> 5, of which waited for: 0 -> 0; matrix products, arithmetic and copies ran while one was open for 0% -> 0% of each run, Pallas kernels for 1% -> 1%
where the time goes in v5:
time: 72.2 us; the launch traced here: 71.9 us
  blocking collectives  43 us (60%)
  Pallas kernels  17.2 us (24%)
  starting transfers between devices  9.53 us (13%)
  local copies, waits for them, and re-layouts  1.97 us (3%)
    all_to_all x1, blocking collectives, local(): lax.all_to_all(copies_of(rows, 2 * seg_count), ('chan', 'seg'), 0, 0, til...  16.3 us
    pallas_call x1, Pallas kernels, fused(): pl.pallas_call(functools.partial(fused_kernel, total_time), in_specs=[SME...  15.5 us
    all_to_all x1, blocking collectives, local(): owned = jnp.sum(lax.all_to_all(slots, 'chan', 0, 0, tiled=True), axis=0)  13.4 us
    all_to_all x1, blocking collectives, local(): gathered = lax.all_to_all(copies, 'seg', 0, 0, tiled=True)  13.3 us
    ppermute x5, starting transfers between devices, exchange(): return lax.ppermute(block, 'chan', [(source(i), i) for i in range(n)])  9.53 us
    unnamed x8, local copies, waits for them, and re-layouts  1.96 us
  transfers between devices with their start and end apart: 5, of which 0 were waited for; matrix products, arithmetic and copies ran while one was open for 0% of the time, Pallas kernels for 1%

profile of v5, /device:TPU:1, one launch (start us, length us, event | category | flops | bytes accessed | tf_op | source)
XLA Modules:
  0.0 71.9 jit_solution(2498890947523741273)
XLA Ops:
  0.0 0.0 copy-start
  0.0 1.0 %copy-done = bf16[128,2048]{1,0:T(8,128)(2,1)S(1)} copy-done((bf16[128,2048]{1,0:T(8,128)(2,1)S(1)}, bf16[128,2048]{1,0:T(8,128)(2,1)}, u32[]{:S(2)}) %copy-start) | copy-done | bytes 524312
  1.0 0.0 copy-start.1
  1.0 0.2 square_sums.1.squares.refs_0_
  1.2 2.5 %collective-permute-start = (f32[1,128]{1,0:T(1,128)S(1)}, f32[1,128]{1,0:T(1,128)S(1)}, u32[]{:S(2)}, u32[]{:S(2)}) collective-permute-start(f32[1,128]{1,0:T(1,128)S(1)} %square_sums.1.squares.refs_0_), channel_id=1, source_target_pairs={{112,0},{0,16},{16,32},{32,48},{48,64},{64,80},{80,96},{96,112},{2... | collective-permute-start | bytes 1544 | tf_op jit(solution)/shard_map/send_squares/ppermute | solution.py:279
  3.8 4.0 %collective-permute-start.1 = (f32[1,128]{1,0:T(1,128)S(1)}, f32[1,128]{1,0:T(1,128)S(1)}, u32[]{:S(2)}, u32[]{:S(2)}) collective-permute-start(f32[1,128]{1,0:T(1,128)S(1)} %square_sums.1.squares.refs_0_), channel_id=1, source_target_pairs={{16,0},{32,16},{48,32},{64,48},{80,64},{96,80},{112,96},{0,112},{1... | collective-permute-start | bytes 1544 | tf_op jit(solution)/shard_map/send_squares/ppermute | solution.py:279
  7.8 0.1 pad_add_fusion.flags
  7.9 0.0 copy-done.1
  7.9 0.0 copy-start.2
  7.9 0.9 %copy-done.2 = s32[2,128,128]{2,1,0:T(8,128)S(1)} copy-done((s32[2,128,128]{2,1,0:T(8,128)S(1)}, s32[2,128,128]{2,1,0:T(8,128)}, u32[]{:S(2)}) %copy-start.2) | copy-done | bytes 131096
  8.8 0.9 %payloads.1 = (bf16[128,1152]{1,0:T(8,128)(2,1)S(1)}, bf16[128,1408]{1,0:T(8,128)(2,1)S(1)}, bf16[128,1280]{1,0:T(8,128)(2,1)S(1)}, bf16[128,1152]{1,0:T(8,128)(2,1)S(1)}) custom-call(s32[3]{0:T(128)S(1)} %pad_add_fusion.flags, f32[1,128]{1,0:T(1,128)S(1)} %square_sums.1.squares.refs_0_, bf16[128,2048]{1,0:T(8,128)(2,1)S(1)} %copy-done.1, ...), custom_call_target="tpu_custom_call" | custom-call | flops 262144 | bytes 2097152 | tf_op jit(solution)/shard_map/payloads/pallas_call | solution.py:210
  9.7 0.0 copy-start.3
  9.7 0.0 collective-permute-done.refs_1_
  9.7 0.0 collective-permute-done.1.refs_2_
  9.7 1.4 %collective-permute-start.4 = (bf16[128,1408]{1,0:T(8,128)(2,1)S(1)}, bf16[128,1408]{1,0:T(8,128)(2,1)S(1)}, u32[]{:S(2)}, u32[]{:S(2)}) collective-permute-start(bf16[128,1408]{1,0:T(8,128)(2,1)S(1)} %get-tuple-element.23), channel_id=1, source_target_pairs={{128,0},{144,16},{160,32},{176,48},{192,64},{208,80},{224,96},{240... | collective-permute-start | bytes 1081352 | tf_op jit(solution)/shard_map/send_blocks/ppermute | solution.py:279
  11.1 1.6 %collective-permute-start.3 = (bf16[128,1280]{1,0:T(8,128)(2,1)S(1)}, bf16[128,1280]{1,0:T(8,128)(2,1)S(1)}, u32[]{:S(2)}, u32[]{:S(2)}) collective-permute-start(bf16[128,1280]{1,0:T(8,128)(2,1)S(1)} %get-tuple-element.22), channel_id=1, source_target_pairs={{16,0},{32,16},{48,32},{64,48},{80,64},{96,80},{112,96},{0,112},{1... | collective-permute-start | bytes 983048 | tf_op jit(solution)/shard_map/send_blocks/ppermute | solution.py:279
  12.7 0.0 collective-permute-start.2
  12.7 16.3 %all_to_all.15.squares = f32[32,3,128]{2,1,0:T(4,128)S(1)} all-to-all(f32[32,3,128]{2,1,0:T(4,128)S(1)} %square_copies.1), channel_id=1, replica_groups={{0,1,2,3,4,5,6,7,8,9,10,11,12,13,14,15,128,129,130,131,132,133,134,135,..., dimensions={0} | all-to-all | bytes 98304 | tf_op jit(solution)/shard_map/energies/all_to_all | solution.py:305
  29.0 0.0 collective-permute-done.2.lower
  29.0 0.0 collective-permute-done.3.upper
  29.0 0.0 collective-permute-done.4.far
  29.0 0.0 copy-done.3
  29.0 15.5 %lags_and_bins.1 = f32[128,256]{1,0:T(8,128)S(1)} custom-call(s32[3]{0:T(128)S(1)} %pad_add_fusion.flags, f32[32,3,128]{2,1,0:T(4,128)S(1)} %all_to_all.15.squares, s32[2,128,128]{2,1,0:T(8,128)S(1)} %copy-done.3, bf16[128,1152]{1,0:T(8,128)(2,1)S(1)} %get-tuple-element.21.stream, bf16[128,1152]{1,0:T(8,128)(2,1)S(1)} %collective-permute-done.2.lower, ...), custom_call_target="tpu_custom_call" | custom-call | flops 9663676416 | bytes 6291456 | tf_op jit(solution)/shard_map/lags_and_bins/pallas_call | solution.py:155
  44.6 13.4 %all_to_all.16 = f32[16,8,256]{2,1,0:T(8,128)S(1)} all-to-all(f32[16,8,256]{2,1,0:T(8,128)S(1)} %bitcast.5), channel_id=1, replica_groups=mesh['chan'=16,'seg'=16] {'chan'}, dimensions={0} | all-to-all | bytes 262144 | tf_op jit(solution)/shard_map/reduce_bins/all_to_all | solution.py:309
  58.1 13.3 %all_to_all.17.gathered = f32[16,8,256]{2,1,0:T(8,128)S(1)} all-to-all(f32[16,8,256]{2,1,0:T(8,128)S(1)} %broadcast_in_dim.2), channel_id=1, replica_groups=mesh['chan'=16,'seg'=16] {'seg'}, dimensions={0} | all-to-all | bytes 262144 | tf_op jit(solution)/shard_map/reduce_bins/all_to_all | solution.py:311
  71.3 0.6 finish.1
  (3 shorter events, 0.0 us)
Async XLA Ops:
  0.0 1.0 %copy-start = (bf16[128,2048]{1,0:T(8,128)(2,1)S(1)}, bf16[128,2048]{1,0:T(8,128)(2,1)}, u32[]{:S(2)}) copy-start(bf16[128,2048]{1,0:T(8,128)(2,1)} %traces.3) | copy-start | bytes 1572868
  1.0 6.8 %copy-start.1 = (bf16[128,2048]{1,0:T(8,128)(2,1)S(1)}, bf16[128,2048]{1,0:T(8,128)(2,1)}, u32[]{:S(2)}) copy-start(bf16[128,2048]{1,0:T(8,128)(2,1)} %traces.3) | copy-start | bytes 1572868
  1.2 8.5 %collective-permute-start = (f32[1,128]{1,0:T(1,128)S(1)}, f32[1,128]{1,0:T(1,128)S(1)}, u32[]{:S(2)}, u32[]{:S(2)}) collective-permute-start(f32[1,128]{1,0:T(1,128)S(1)} %square_sums.1.squares.refs_0_), channel_id=1, source_target_pairs={{112,0},{0,16},{16,32},{32,48},{48,64},{64,80},{80,96},{96,112},{2... | collective-permute-start | bytes 1544 | tf_op jit(solution)/shard_map/send_squares/ppermute | solution.py:279
  3.8 6.0 %collective-permute-start.1 = (f32[1,128]{1,0:T(1,128)S(1)}, f32[1,128]{1,0:T(1,128)S(1)}, u32[]{:S(2)}, u32[]{:S(2)}) collective-permute-start(f32[1,128]{1,0:T(1,128)S(1)} %square_sums.1.squares.refs_0_), channel_id=1, source_target_pairs={{16,0},{32,16},{48,32},{64,48},{80,64},{96,80},{112,96},{0,112},{1... | collective-permute-start | bytes 1544 | tf_op jit(solution)/shard_map/send_squares/ppermute | solution.py:279
  7.9 0.9 %copy-start.2 = (s32[2,128,128]{2,1,0:T(8,128)S(1)}, s32[2,128,128]{2,1,0:T(8,128)}, u32[]{:S(2)}) copy-start(s32[2,128,128]{2,1,0:T(8,128)} %bins_ref.1) | copy-start | bytes 393220
  9.7 19.3 %copy-start.3 = (s32[2,128,128]{2,1,0:T(8,128)S(1)}, s32[2,128,128]{2,1,0:T(8,128)}, u32[]{:S(2)}) copy-start(s32[2,128,128]{2,1,0:T(8,128)} %bins_ref.1) | copy-start | bytes 393220
  9.7 19.3 %collective-permute-start.4 = (bf16[128,1408]{1,0:T(8,128)(2,1)S(1)}, bf16[128,1408]{1,0:T(8,128)(2,1)S(1)}, u32[]{:S(2)}, u32[]{:S(2)}) collective-permute-start(bf16[128,1408]{1,0:T(8,128)(2,1)S(1)} %get-tuple-element.23), channel_id=1, source_target_pairs={{128,0},{144,16},{160,32},{176,48},{192,64},{208,80},{224,96},{240... | collective-permute-start | bytes 1081352 | tf_op jit(solution)/shard_map/send_blocks/ppermute | solution.py:279
  11.1 17.9 %collective-permute-start.3 = (bf16[128,1280]{1,0:T(8,128)(2,1)S(1)}, bf16[128,1280]{1,0:T(8,128)(2,1)S(1)}, u32[]{:S(2)}, u32[]{:S(2)}) collective-permute-start(bf16[128,1280]{1,0:T(8,128)(2,1)S(1)} %get-tuple-element.22), channel_id=1, source_target_pairs={{16,0},{32,16},{48,32},{64,48},{80,64},{96,80},{112,96},{0,112},{1... | collective-permute-start | bytes 983048 | tf_op jit(solution)/shard_map/send_blocks/ppermute | solution.py:279
  12.7 16.3 %collective-permute-start.2 = (bf16[128,1152]{1,0:T(8,128)(2,1)S(1)}, bf16[128,1152]{1,0:T(8,128)(2,1)S(1)}, u32[]{:S(2)}, u32[]{:S(2)}) collective-permute-start(bf16[128,1152]{1,0:T(8,128)(2,1)S(1)} %get-tuple-element.21.stream), channel_id=1, source_target_pairs={{112,0},{0,16},{16,32},{32,48},{48,64},{64,80},{80,96},{96,112},{2... | collective-permute-start | bytes 884744 | tf_op jit(solution)/shard_map/send_blocks/ppermute | solution.py:279

commit v6 on v5

--- a/solution.py
+++ b/solution.py
@@ -85,9 +85,9 @@
         home = jnp.where(flags[0] == 1, high, low)
         inverse_rms = lambda v: lax.rsqrt(v / total_time + EPSILON)
         near = inverse_rms(home)
-        own, far_scale = near[0:1], inverse_rms(jnp.where(flags[0] == 1, low, high)[0:1])
+        own, far_scale = near[:, :CB], inverse_rms(jnp.where(flags[0] == 1, low, high)[:, :CB])
         held = (far_scale, jnp.where(first, own, far_scale), jnp.where(last, own, far_scale))
-        for t, streamed in enumerate((own, near[1:2], near[2:3])):
+        for t, streamed in enumerate((own, near[:, CB:2 * CB], near[:, 2 * CB:])):
             column = jnp.transpose(jnp.broadcast_to(streamed, (CB, CB)))
             pair_scale[t] = column * (held[t] * (1.0 / math.sqrt(total_time)))
         sets = (far[:, W:W + CB].astype(F32), bins_ref[0].astype(F32),
@@ -240,7 +240,7 @@
 
 
 def copies_kernel(*refs):
-    rows = jnp.concatenate([ref[...] for ref in refs[:-1]], 0)
+    rows = jnp.concatenate([ref[...] for ref in refs[:-1]], 1)
     refs[-1][...] = jnp.broadcast_to(rows[None], refs[-1].shape)
 
 
@@ -249,7 +249,7 @@
         copies_kernel,
         in_specs=[VMEM] * len(rows),
         out_specs=VMEM,
-        out_shape=jax.ShapeDtypeStruct((count, len(rows), CB), F32),
+        out_shape=jax.ShapeDtypeStruct((count, 1, len(rows) * CB), F32),
         compiler_params=pltpu.CompilerParams(vmem_limit_bytes=2 << 20),
         cost_estimate=pl.CostEstimate(flops=1 << 12, bytes_accessed=1 << 15, transcendentals=0),
         name="square_copies",

time: 72.2 us -> 72.2 us (level)
  no operation moved by 1% of the time
where the time goes in v6:
time: 72.2 us; the launch traced here: 71.9 us
  blocking collectives  43 us (60%)
  Pallas kernels  17.2 us (24%)
  starting transfers between devices  9.53 us (13%)
  local copies, waits for them, and re-layouts  1.97 us (3%)
    all_to_all x1, blocking collectives, local(): lax.all_to_all(copies_of(rows, 2 * seg_count), ('chan', 'seg'), 0, 0, til...  16.3 us
    pallas_call x1, Pallas kernels, fused(): pl.pallas_call(functools.partial(fused_kernel, total_time), in_specs=[SME...  15.5 us
    all_to_all x1, blocking collectives, local(): owned = jnp.sum(lax.all_to_all(slots, 'chan', 0, 0, tiled=True), axis=0)  13.5 us
    all_to_all x1, blocking collectives, local(): gathered = lax.all_to_all(copies, 'seg', 0, 0, tiled=True)  13.3 us
    ppermute x5, starting transfers between devices, exchange(): return lax.ppermute(block, 'chan', [(source(i), i) for i in range(n)])  9.53 us
    unnamed x8, local copies, waits for them, and re-layouts  1.96 us
  transfers between devices with their start and end apart: 5, of which 0 were waited for; matrix products, arithmetic and copies ran while one was open for 0% of the time, Pallas kernels for 1%

profile of v6, /device:TPU:1, one launch (start us, length us, event | category | flops | bytes accessed | tf_op | source)
XLA Modules:
  0.0 71.9 jit_solution(12557675637139302043)
XLA Ops:
  0.0 0.0 copy-start
  0.0 1.0 %copy-done = bf16[128,2048]{1,0:T(8,128)(2,1)S(1)} copy-done((bf16[128,2048]{1,0:T(8,128)(2,1)S(1)}, bf16[128,2048]{1,0:T(8,128)(2,1)}, u32[]{:S(2)}) %copy-start) | copy-done | bytes 524312
  1.0 0.0 copy-start.1
  1.0 0.2 square_sums.1.squares.refs_0_
  1.2 2.5 %collective-permute-start = (f32[1,128]{1,0:T(1,128)S(1)}, f32[1,128]{1,0:T(1,128)S(1)}, u32[]{:S(2)}, u32[]{:S(2)}) collective-permute-start(f32[1,128]{1,0:T(1,128)S(1)} %square_sums.1.squares.refs_0_), channel_id=1, source_target_pairs={{112,0},{0,16},{16,32},{32,48},{48,64},{64,80},{80,96},{96,112},{2... | collective-permute-start | bytes 1544 | tf_op jit(solution)/shard_map/send_squares/ppermute | solution.py:279
  3.8 4.0 %collective-permute-start.1 = (f32[1,128]{1,0:T(1,128)S(1)}, f32[1,128]{1,0:T(1,128)S(1)}, u32[]{:S(2)}, u32[]{:S(2)}) collective-permute-start(f32[1,128]{1,0:T(1,128)S(1)} %square_sums.1.squares.refs_0_), channel_id=1, source_target_pairs={{16,0},{32,16},{48,32},{64,48},{80,64},{96,80},{112,96},{0,112},{1... | collective-permute-start | bytes 1544 | tf_op jit(solution)/shard_map/send_squares/ppermute | solution.py:279
  7.8 0.1 pad_add_fusion.flags
  7.9 0.0 copy-done.1
  7.9 0.0 copy-start.2
  7.9 0.9 %copy-done.2 = s32[2,128,128]{2,1,0:T(8,128)S(1)} copy-done((s32[2,128,128]{2,1,0:T(8,128)S(1)}, s32[2,128,128]{2,1,0:T(8,128)}, u32[]{:S(2)}) %copy-start.2) | copy-done | bytes 131096
  8.8 0.9 %payloads.1 = (bf16[128,1152]{1,0:T(8,128)(2,1)S(1)}, bf16[128,1408]{1,0:T(8,128)(2,1)S(1)}, bf16[128,1280]{1,0:T(8,128)(2,1)S(1)}, bf16[128,1152]{1,0:T(8,128)(2,1)S(1)}) custom-call(s32[3]{0:T(128)S(1)} %pad_add_fusion.flags, f32[1,128]{1,0:T(1,128)S(1)} %square_sums.1.squares.refs_0_, bf16[128,2048]{1,0:T(8,128)(2,1)S(1)} %copy-done.1, ...), custom_call_target="tpu_custom_call" | custom-call | flops 262144 | bytes 2097152 | tf_op jit(solution)/shard_map/payloads/pallas_call | solution.py:210
  9.7 0.0 copy-start.3
  9.7 0.0 collective-permute-done.refs_1_
  9.7 0.0 collective-permute-done.1.refs_2_
  9.7 1.4 %collective-permute-start.4 = (bf16[128,1408]{1,0:T(8,128)(2,1)S(1)}, bf16[128,1408]{1,0:T(8,128)(2,1)S(1)}, u32[]{:S(2)}, u32[]{:S(2)}) collective-permute-start(bf16[128,1408]{1,0:T(8,128)(2,1)S(1)} %get-tuple-element.23), channel_id=1, source_target_pairs={{128,0},{144,16},{160,32},{176,48},{192,64},{208,80},{224,96},{240... | collective-permute-start | bytes 1081352 | tf_op jit(solution)/shard_map/send_blocks/ppermute | solution.py:279
  11.1 1.6 %collective-permute-start.3 = (bf16[128,1280]{1,0:T(8,128)(2,1)S(1)}, bf16[128,1280]{1,0:T(8,128)(2,1)S(1)}, u32[]{:S(2)}, u32[]{:S(2)}) collective-permute-start(bf16[128,1280]{1,0:T(8,128)(2,1)S(1)} %get-tuple-element.22), channel_id=1, source_target_pairs={{16,0},{32,16},{48,32},{64,48},{80,64},{96,80},{112,96},{0,112},{1... | collective-permute-start | bytes 983048 | tf_op jit(solution)/shard_map/send_blocks/ppermute | solution.py:279
  12.7 0.0 collective-permute-start.2
  12.7 16.3 %all_to_all.15.squares = f32[32,1,384]{2,1,0:T(1,128)S(1)} all-to-all(f32[32,1,384]{2,1,0:T(1,128)S(1)} %square_copies.1), channel_id=1, replica_groups={{0,1,2,3,4,5,6,7,8,9,10,11,12,13,14,15,128,129,130,131,132,133,134,135,..., dimensions={0} | all-to-all | bytes 98304 | tf_op jit(solution)/shard_map/energies/all_to_all | solution.py:305
  29.0 0.0 collective-permute-done.2.lower
  29.0 0.0 collective-permute-done.3.upper
  29.0 0.0 collective-permute-done.4.far
  29.0 0.0 copy-done.3
  29.0 15.5 %lags_and_bins.1 = f32[128,256]{1,0:T(8,128)S(1)} custom-call(s32[3]{0:T(128)S(1)} %pad_add_fusion.flags, f32[32,1,384]{2,1,0:T(1,128)S(1)} %all_to_all.15.squares, s32[2,128,128]{2,1,0:T(8,128)S(1)} %copy-done.3, bf16[128,1152]{1,0:T(8,128)(2,1)S(1)} %get-tuple-element.21.stream, bf16[128,1152]{1,0:T(8,128)(2,1)S(1)} %collective-permute-done.2.lower, ...), custom_call_target="tpu_custom_call" | custom-call | flops 9663676416 | bytes 6291456 | tf_op jit(solution)/shard_map/lags_and_bins/pallas_call | solution.py:155
  44.5 13.5 %all_to_all.16 = f32[16,8,256]{2,1,0:T(8,128)S(1)} all-to-all(f32[16,8,256]{2,1,0:T(8,128)S(1)} %bitcast.5), channel_id=1, replica_groups=mesh['chan'=16,'seg'=16] {'chan'}, dimensions={0} | all-to-all | bytes 262144 | tf_op jit(solution)/shard_map/reduce_bins/all_to_all | solution.py:309
  58.0 13.3 %all_to_all.17.gathered = f32[16,8,256]{2,1,0:T(8,128)S(1)} all-to-all(f32[16,8,256]{2,1,0:T(8,128)S(1)} %broadcast_in_dim.2), channel_id=1, replica_groups=mesh['chan'=16,'seg'=16] {'seg'}, dimensions={0} | all-to-all | bytes 262144 | tf_op jit(solution)/shard_map/reduce_bins/all_to_all | solution.py:311
  71.3 0.6 finish.1
  (3 shorter events, 0.0 us)
Async XLA Ops:
  0.0 1.0 %copy-start = (bf16[128,2048]{1,0:T(8,128)(2,1)S(1)}, bf16[128,2048]{1,0:T(8,128)(2,1)}, u32[]{:S(2)}) copy-start(bf16[128,2048]{1,0:T(8,128)(2,1)} %traces.3) | copy-start | bytes 1572868
  1.0 6.8 %copy-start.1 = (bf16[128,2048]{1,0:T(8,128)(2,1)S(1)}, bf16[128,2048]{1,0:T(8,128)(2,1)}, u32[]{:S(2)}) copy-start(bf16[128,2048]{1,0:T(8,128)(2,1)} %traces.3) | copy-start | bytes 1572868
  1.2 8.5 %collective-permute-start = (f32[1,128]{1,0:T(1,128)S(1)}, f32[1,128]{1,0:T(1,128)S(1)}, u32[]{:S(2)}, u32[]{:S(2)}) collective-permute-start(f32[1,128]{1,0:T(1,128)S(1)} %square_sums.1.squares.refs_0_), channel_id=1, source_target_pairs={{112,0},{0,16},{16,32},{32,48},{48,64},{64,80},{80,96},{96,112},{2... | collective-permute-start | bytes 1544 | tf_op jit(solution)/shard_map/send_squares/ppermute | solution.py:279
  3.8 6.0 %collective-permute-start.1 = (f32[1,128]{1,0:T(1,128)S(1)}, f32[1,128]{1,0:T(1,128)S(1)}, u32[]{:S(2)}, u32[]{:S(2)}) collective-permute-start(f32[1,128]{1,0:T(1,128)S(1)} %square_sums.1.squares.refs_0_), channel_id=1, source_target_pairs={{16,0},{32,16},{48,32},{64,48},{80,64},{96,80},{112,96},{0,112},{1... | collective-permute-start | bytes 1544 | tf_op jit(solution)/shard_map/send_squares/ppermute | solution.py:279
  7.9 0.9 %copy-start.2 = (s32[2,128,128]{2,1,0:T(8,128)S(1)}, s32[2,128,128]{2,1,0:T(8,128)}, u32[]{:S(2)}) copy-start(s32[2,128,128]{2,1,0:T(8,128)} %bins_ref.1) | copy-start | bytes 393220
  9.7 19.3 %copy-start.3 = (s32[2,128,128]{2,1,0:T(8,128)S(1)}, s32[2,128,128]{2,1,0:T(8,128)}, u32[]{:S(2)}) copy-start(s32[2,128,128]{2,1,0:T(8,128)} %bins_ref.1) | copy-start | bytes 393220
  9.7 19.3 %collective-permute-start.4 = (bf16[128,1408]{1,0:T(8,128)(2,1)S(1)}, bf16[128,1408]{1,0:T(8,128)(2,1)S(1)}, u32[]{:S(2)}, u32[]{:S(2)}) collective-permute-start(bf16[128,1408]{1,0:T(8,128)(2,1)S(1)} %get-tuple-element.23), channel_id=1, source_target_pairs={{128,0},{144,16},{160,32},{176,48},{192,64},{208,80},{224,96},{240... | collective-permute-start | bytes 1081352 | tf_op jit(solution)/shard_map/send_blocks/ppermute | solution.py:279
  11.1 17.9 %collective-permute-start.3 = (bf16[128,1280]{1,0:T(8,128)(2,1)S(1)}, bf16[128,1280]{1,0:T(8,128)(2,1)S(1)}, u32[]{:S(2)}, u32[]{:S(2)}) collective-permute-start(bf16[128,1280]{1,0:T(8,128)(2,1)S(1)} %get-tuple-element.22), channel_id=1, source_target_pairs={{16,0},{32,16},{48,32},{64,48},{80,64},{96,80},{112,96},{0,112},{1... | collective-permute-start | bytes 983048 | tf_op jit(solution)/shard_map/send_blocks/ppermute | solution.py:279
  12.7 16.3 %collective-permute-start.2 = (bf16[128,1152]{1,0:T(8,128)(2,1)S(1)}, bf16[128,1152]{1,0:T(8,128)(2,1)S(1)}, u32[]{:S(2)}, u32[]{:S(2)}) collective-permute-start(bf16[128,1152]{1,0:T(8,128)(2,1)S(1)} %get-tuple-element.21.stream), channel_id=1, source_target_pairs={{112,0},{0,16},{16,32},{32,48},{48,64},{64,80},{80,96},{96,112},{2... | collective-permute-start | bytes 884744 | tf_op jit(solution)/shard_map/send_blocks/ppermute | solution.py:279
